TPU v7x, 32 devices: a whole 2x2x4 slice. The times are simulated.
32 devices in a mesh: expert: 8 (over z, x), tensor: 4 (over y, core).
Axes of the slice: x: 2, y: 2, z: 4, core: 2. Of those that a mesh axis runs over, the one named last changes fastest.
Arguments:
- hidden_in: bfloat16 [8192, 768], P('expert'), may hold values from -6 to 6
- norm_attn: float32 [768], replicated, may hold values from 0.5 to 1.5
- w_query: bfloat16 [768, 768], P(None, 'tensor'), may hold values from -0.21875 to 0.21875
- w_key: bfloat16 [768, 768], P(None, 'tensor'), may hold values from -0.21875 to 0.21875
- w_value: bfloat16 [768, 768], P(None, 'tensor'), may hold values from -0.21875 to 0.21875
- w_out: bfloat16 [768, 768], P('tensor'), may hold values from -0.625 to 0.625
- norm_ffn: float32 [768], replicated, may hold values from 0.5 to 1.5
- w_router: bfloat16 [768, 8], replicated, may hold values from -0.15625 to 0.15625
- shared_gate: bfloat16 [768, 2048], P(None, 'tensor'), may hold values from -0.21875 to 0.21875
- shared_up: bfloat16 [768, 2048], P(None, 'tensor'), may hold values from -0.21875 to 0.21875
- shared_down: bfloat16 [2048, 768], P('tensor'), may hold values from -0.125 to 0.125
- expert_gate: bfloat16 [8, 768, 2048], P('expert', None, 'tensor'), may hold values from -0.21875 to 0.21875
- expert_up: bfloat16 [8, 768, 2048], P('expert', None, 'tensor'), may hold values from -0.21875 to 0.21875
- expert_down: bfloat16 [8, 2048, 768], P('expert', 'tensor'), may hold values from -0.125 to 0.125
- segment: int32 [8192], P('expert'), may hold values from 0 to 8, as said below
- routes: int32 [8192, 2], P('expert'), may hold values from 0 to 7, as said below
- slots: int32 [8192, 2], P('expert'), may hold values from 0 to 384, as said below
- teacher: bfloat16 [8192, 768], P('expert', 'tensor'), may hold values from -6 to 6
Outputs:
- loss: float32 [], replicated
- activations: bfloat16 [8192, 768], P('expert', 'tensor')
- grad_input: float32 [8192, 768], P('expert', 'tensor')
- grad_norm_attn: float32 [768], replicated
- grad_query: float32 [768, 768], P(None, 'tensor')
- grad_key: float32 [768, 768], P(None, 'tensor')
- grad_value: float32 [768, 768], P(None, 'tensor')
- grad_out: float32 [768, 768], P('tensor')
- grad_norm_ffn: float32 [768], replicated
- grad_router: float32 [768, 8], replicated
- grad_shared_gate: float32 [768, 2048], P(None, 'tensor')
- grad_shared_up: float32 [768, 2048], P(None, 'tensor')
- grad_shared_down: float32 [2048, 768], P('tensor')
- grad_expert_gate: float32 [8, 768, 2048], P('expert', None, 'tensor')
- grad_expert_up: float32 [8, 768, 2048], P('expert', None, 'tensor')
- grad_expert_down: float32 [8, 2048, 768], P('expert', 'tensor')
Inputs may be any that keep to these rules, and one draw needn't show every extreme that they name: `segment`: each run of 1024 consecutive tokens is one sequence: document ids 1, 2, ... never falling along it (some documents may be empty), then padding with id 0 at its end, at most 128 tokens. `routes`: A token's two experts differ. `slots`: within one sequence, the pairs that name an expert carry the rows 0, 1, 2, ... in some order, and those beyond 384 carry 384 (dropped); in every draw some expert is named by more than 384 pairs of every sequence.
All inputs are finite; a program needn't handle non-finite values.
Results may differ from a plain program's by a relative error of at most 0.02.
Values may be sent and summed in bfloat16 or wider, within the bound.
A program may use at most 256 MiB of HBM per device.

v0:
```python
import jax
import jax.numpy as jnp
from jax import lax
from jax.sharding import PartitionSpec as P

HD = 64


eps_norm = 1e-06


def rope_tables(length, head_dim):
    half = head_dim // 2
    freqs = 10000.0 ** (-2.0 * jnp.arange(half, dtype=jnp.float32) / head_dim)
    angles = jnp.arange(length, dtype=jnp.float32)[:, None] * freqs[None, :]
    return (jnp.cos(angles), jnp.sin(angles))


def rotate(vec, cosine, sine):
    half = vec.shape[-1] // 2
    first = vec[..., :half]
    second = vec[..., half:]
    return jnp.concatenate(
        [first * cosine - second * sine, second * cosine + first * sine], axis=-1
    )


def rotate_back(grad, cosine, sine):
    half = grad.shape[-1] // 2
    first = grad[..., :half]
    second = grad[..., half:]
    return jnp.concatenate(
        [first * cosine + second * sine, second * cosine - first * sine], axis=-1
    )


def silu_slope(value):
    sigma = jax.nn.sigmoid(value)
    return sigma * (1.0 + value * (1.0 - sigma))


def norm_back(grad, value, scale, gain):
    scaled = grad * gain
    inner = jnp.mean(scaled * value, axis=-1, keepdims=True)
    return (
        scale * scaled - value * scale * scale * scale * inner,
        jnp.sum(grad * value * scale, axis=0),
    )


def split_heads(flat, heads):
    return flat.reshape(flat.shape[0], heads, -1).transpose(1, 0, 2)


def merge_heads(stacked):
    return stacked.transpose(1, 0, 2).reshape(stacked.shape[1], -1)


def block_scores(q_block, keys, segment, start, block):
    length = keys.shape[1]
    scale = keys.shape[2] ** (-0.5)
    seg_block = lax.dynamic_slice_in_dim(segment, start, block, 0)
    places = jnp.arange(length)
    rows_at = start + jnp.arange(block)
    allowed = (seg_block[:, None] == segment[None, :]) & (places[None, :] <= rows_at[:, None])
    scores = jnp.einsum("hqd,hkd->hqk", q_block, keys, preferred_element_type=jnp.float32) * scale
    return (jnp.where(allowed[None], scores, -1e30), allowed)


def attend_forward(query, keys, values, segment, block):
    heads, length, width = query.shape

    def one_block(start):
        q_block = lax.dynamic_slice_in_dim(query, start, block, 1)
        scores, allowed = block_scores(q_block, keys, segment, start, block)
        top = jnp.max(scores, axis=-1, keepdims=True)
        expo = jnp.exp(scores - top)
        total = jnp.sum(expo, axis=-1, keepdims=True)
        prob = (expo / total).astype(jnp.bfloat16)
        mixed = jnp.einsum("hqk,hkd->hqd", prob, values, preferred_element_type=jnp.float32)
        return (mixed, (top + jnp.log(total))[..., 0])

    starts = jnp.arange(length // block) * block
    mixed, summary = lax.map(one_block, starts)
    mixed = mixed.transpose(1, 0, 2, 3).reshape(heads, length, width)
    summary = summary.transpose(1, 0, 2).reshape(heads, length)
    return (mixed, summary)


def attend_backward(query, keys, values, segment, summary, grad_mixed, block):
    heads, length, width = query.shape
    scale = width ** (-0.5)

    def one_block(carry, start):
        grad_keys, grad_values = carry
        q_block = lax.dynamic_slice_in_dim(query, start, block, 1)
        scores, allowed = block_scores(q_block, keys, segment, start, block)
        sum_block = lax.dynamic_slice_in_dim(summary, start, block, 1)
        prob = jnp.where(allowed[None], jnp.exp(scores - sum_block[..., None]), 0.0)
        grad_block = lax.dynamic_slice_in_dim(grad_mixed, start, block, 1)
        grad_prob = jnp.einsum(
            "hqd,hkd->hqk", grad_block, values, preferred_element_type=jnp.float32
        )
        inner = jnp.sum(prob * grad_prob, axis=-1, keepdims=True)
        grad_scores = (prob * (grad_prob - inner)).astype(jnp.bfloat16)
        grad_q = (
            jnp.einsum("hqk,hkd->hqd", grad_scores, keys, preferred_element_type=jnp.float32)
            * scale
        )
        grad_keys = (
            grad_keys
            + jnp.einsum("hqk,hqd->hkd", grad_scores, q_block, preferred_element_type=jnp.float32)
            * scale
        )
        grad_values = grad_values + jnp.einsum(
            "hqk,hqd->hkd",
            prob.astype(jnp.bfloat16),
            grad_block,
            preferred_element_type=jnp.float32,
        )
        return ((grad_keys, grad_values), grad_q)

    starts = jnp.arange(length // block) * block
    zeros = jnp.zeros((heads, length, width), jnp.float32)
    (grad_keys, grad_values), grad_q = lax.scan(one_block, (zeros, zeros), starts)
    grad_q = grad_q.transpose(1, 0, 2, 3).reshape(heads, length, width)
    return (grad_q, grad_keys, grad_values)


def body(
    hidden_in,
    norm_attn,
    w_query,
    w_key,
    w_value,
    w_out,
    norm_ffn,
    w_router,
    shared_gate,
    shared_up,
    shared_down,
    expert_gate,
    expert_up,
    expert_down,
    segment,
    routes,
    slots,
    teacher,
):
    length, width = hidden_in.shape
    groups = lax.axis_size("expert")
    members = lax.axis_size("tensor")
    quarter = width // members
    offset = lax.axis_index("tensor") * quarter
    experts = w_router.shape[1]
    capacity = 3 * length // groups
    tokens = length * groups
    local_heads = w_query.shape[1] // HD
    block = min(512, length)
    inputs = hidden_in.astype(jnp.float32)
    scale_one = lax.rsqrt(jnp.mean(inputs * inputs, axis=-1, keepdims=True) + eps_norm)
    normed_one = (inputs * scale_one * norm_attn).astype(jnp.bfloat16)
    cosine, sine = rope_tables(length, HD)
    query = rotate(
        split_heads(jnp.dot(normed_one, w_query, preferred_element_type=jnp.float32), local_heads),
        cosine,
        sine,
    ).astype(jnp.bfloat16)
    keys = rotate(
        split_heads(jnp.dot(normed_one, w_key, preferred_element_type=jnp.float32), local_heads),
        cosine,
        sine,
    ).astype(jnp.bfloat16)
    values = split_heads(
        jnp.dot(normed_one, w_value, preferred_element_type=jnp.float32), local_heads
    ).astype(jnp.bfloat16)
    mixed, summary = attend_forward(query, keys, values, segment, block)
    mixed_low = merge_heads(mixed).astype(jnp.bfloat16)
    attention = lax.psum(
        jnp.dot(mixed_low, w_out, preferred_element_type=jnp.float32).astype(jnp.bfloat16), "tensor"
    ).astype(jnp.float32)
    residual = inputs + attention
    scale_two = lax.rsqrt(jnp.mean(residual * residual, axis=-1, keepdims=True) + eps_norm)
    normed_two = (residual * scale_two * norm_ffn).astype(jnp.bfloat16)
    logits = jnp.dot(normed_two, w_router, preferred_element_type=jnp.float32)
    onehot = (routes[:, :, None] == jnp.arange(experts, dtype=jnp.int32)[None, None, :]).astype(
        jnp.float32
    )
    chosen = jnp.einsum("te,tke->tk", logits, onehot)
    gates = jax.nn.softmax(chosen, axis=1)
    side_pre = jnp.dot(normed_two, shared_gate, preferred_element_type=jnp.float32)
    side_lin = jnp.dot(normed_two, shared_up, preferred_element_type=jnp.float32)
    side_hidden = (jax.nn.silu(side_pre) * side_lin).astype(jnp.bfloat16)
    side_part = jnp.dot(side_hidden, shared_down, preferred_element_type=jnp.float32)
    kept = slots < capacity
    target = jnp.where(kept, routes * capacity + slots, experts * capacity).reshape(-1)
    pair_rows = jnp.broadcast_to(normed_two[:, None, :], (length, 2, width)).reshape(
        2 * length, width
    )
    outgoing = jnp.zeros((experts * capacity + 1, width), jnp.bfloat16).at[target].set(pair_rows)
    outgoing = outgoing[:-1].reshape(experts, capacity, width)
    arrived = lax.all_to_all(outgoing, "expert", split_axis=0, concat_axis=0, tiled=True)
    rows_in = arrived.reshape(groups * capacity, width)
    expert_pre = jnp.dot(rows_in, expert_gate[0], preferred_element_type=jnp.float32)
    expert_lin = jnp.dot(rows_in, expert_up[0], preferred_element_type=jnp.float32)
    expert_hidden = (jax.nn.silu(expert_pre) * expert_lin).astype(jnp.bfloat16)
    expert_part = jnp.dot(
        expert_hidden, expert_down[0], preferred_element_type=jnp.float32
    ).reshape(groups, capacity, width)
    expert_sum, side_sum = (
        lax.psum_scatter(
            expert_part.astype(jnp.bfloat16), "tensor", scatter_dimension=2, tiled=True
        ).astype(jnp.float32),
        lax.psum_scatter(
            side_part.astype(jnp.bfloat16), "tensor", scatter_dimension=1, tiled=True
        ).astype(jnp.float32),
    )
    returned = lax.all_to_all(
        expert_sum.astype(jnp.bfloat16), "expert", split_axis=0, concat_axis=0, tiled=True
    )
    lookup = jnp.concatenate(
        [returned.reshape(experts * capacity, quarter), jnp.zeros((1, quarter), jnp.bfloat16)],
        axis=0,
    )
    fetched = lookup[target].reshape(length, 2, quarter).astype(jnp.float32)
    mixture = jnp.sum(gates[:, :, None] * fetched, axis=1)
    residual_part = lax.dynamic_slice_in_dim(residual, offset, quarter, 1)
    final = residual_part + side_sum + mixture
    valid = (segment != 0).astype(jnp.float32)
    error = final - teacher.astype(jnp.float32)
    square_sum, count = lax.psum(
        (jnp.sum(valid[:, None] * error * error), jnp.sum(valid) / members), ("expert", "tensor")
    )
    loss = square_sum / (count * width)
    grad_final = error * valid[:, None] * (2.0 * tokens / count)
    grad_full = lax.all_gather(
        grad_final.astype(jnp.bfloat16), "tensor", axis=1, tiled=True
    ).astype(grad_final.dtype)
    grad_low = grad_full.astype(jnp.bfloat16)
    gate_part = jnp.sum(grad_final[:, None, :] * fetched, axis=2)
    pair_grad = (
        (gates[:, :, None] * grad_final[:, None, :])
        .astype(jnp.bfloat16)
        .reshape(2 * length, quarter)
    )
    grad_buffer = (
        jnp.zeros((experts * capacity + 1, quarter), jnp.bfloat16).at[target].set(pair_grad)
    )
    grad_buffer = grad_buffer[:-1].reshape(experts, capacity, quarter)
    grad_arrived = lax.all_to_all(grad_buffer, "expert", split_axis=0, concat_axis=0, tiled=True)
    grad_rows = lax.all_gather(grad_arrived, "tensor", axis=2, tiled=True).reshape(
        groups * capacity, width
    )
    grad_expert_hidden = jnp.dot(grad_rows, expert_down[0].T, preferred_element_type=jnp.float32)
    grad_expert_down = jnp.dot(expert_hidden.T, grad_rows, preferred_element_type=jnp.float32)
    pre_grad = (grad_expert_hidden * expert_lin * silu_slope(expert_pre)).astype(jnp.bfloat16)
    lin_grad = (grad_expert_hidden * jax.nn.silu(expert_pre)).astype(jnp.bfloat16)
    grad_expert_gate = jnp.dot(rows_in.T, pre_grad, preferred_element_type=jnp.float32)
    grad_expert_up = jnp.dot(rows_in.T, lin_grad, preferred_element_type=jnp.float32)
    grad_rows_in = jnp.dot(pre_grad, expert_gate[0].T, preferred_element_type=jnp.float32)
    grad_rows_in = grad_rows_in + jnp.dot(
        lin_grad, expert_up[0].T, preferred_element_type=jnp.float32
    )
    grad_share = lax.psum_scatter(
        grad_rows_in.reshape(groups, capacity, width).astype(jnp.bfloat16),
        "tensor",
        scatter_dimension=2,
        tiled=True,
    )
    grad_back = lax.all_to_all(grad_share, "expert", split_axis=0, concat_axis=0, tiled=True)
    grad_lookup = jnp.concatenate(
        [grad_back.reshape(experts * capacity, quarter), jnp.zeros((1, quarter), jnp.bfloat16)],
        axis=0,
    )
    grad_dispatch = jnp.sum(
        grad_lookup[target].reshape(length, 2, quarter).astype(jnp.float32), axis=1
    )
    grad_side_hidden = jnp.dot(grad_low, shared_down.T, preferred_element_type=jnp.float32)
    grad_shared_down = jnp.dot(side_hidden.T, grad_low, preferred_element_type=jnp.float32)
    side_pre_grad = (grad_side_hidden * side_lin * silu_slope(side_pre)).astype(jnp.bfloat16)
    side_lin_grad = (grad_side_hidden * jax.nn.silu(side_pre)).astype(jnp.bfloat16)
    grad_shared_gate = jnp.dot(normed_two.T, side_pre_grad, preferred_element_type=jnp.float32)
    grad_shared_up = jnp.dot(normed_two.T, side_lin_grad, preferred_element_type=jnp.float32)
    grad_normed = jnp.dot(side_pre_grad, shared_gate.T, preferred_element_type=jnp.float32)
    grad_normed = grad_normed + jnp.dot(
        side_lin_grad, shared_up.T, preferred_element_type=jnp.float32
    )
    own_columns = lax.dynamic_slice_in_dim(grad_normed, offset, quarter, 1) + grad_dispatch
    grad_normed = lax.dynamic_update_slice_in_dim(grad_normed, own_columns, offset, 1)
    grad_normed, grad_gates = (
        lax.psum(grad_normed.astype(jnp.bfloat16), "tensor").astype(jnp.float32),
        lax.psum(gate_part.astype(jnp.bfloat16), "tensor").astype(jnp.float32),
    )
    grad_chosen = gates * (grad_gates - jnp.sum(gates * grad_gates, axis=1, keepdims=True))
    grad_logits = jnp.einsum("tk,tke->te", grad_chosen, onehot).astype(jnp.bfloat16)
    grad_router = jnp.dot(normed_two.T, grad_logits, preferred_element_type=jnp.float32)
    grad_normed = grad_normed + jnp.dot(grad_logits, w_router.T, preferred_element_type=jnp.float32)
    grad_through, grad_norm_ffn = norm_back(grad_normed, residual, scale_two, norm_ffn)
    grad_residual = grad_full + grad_through
    grad_attention = grad_residual.astype(jnp.bfloat16)
    grad_w_out = jnp.dot(mixed_low.T, grad_attention, preferred_element_type=jnp.float32)
    grad_mixed = split_heads(
        jnp.dot(grad_attention, w_out.T, preferred_element_type=jnp.float32), local_heads
    ).astype(jnp.bfloat16)
    grad_q, grad_k, grad_v = attend_backward(
        query, keys, values, segment, summary, grad_mixed, block
    )
    grad_q = merge_heads(rotate_back(grad_q, cosine, sine)).astype(jnp.bfloat16)
    grad_k = merge_heads(rotate_back(grad_k, cosine, sine)).astype(jnp.bfloat16)
    grad_v = merge_heads(grad_v).astype(jnp.bfloat16)
    grad_w_query = jnp.dot(normed_one.T, grad_q, preferred_element_type=jnp.float32)
    grad_w_key = jnp.dot(normed_one.T, grad_k, preferred_element_type=jnp.float32)
    grad_w_value = jnp.dot(normed_one.T, grad_v, preferred_element_type=jnp.float32)
    grad_normed_one = jnp.dot(grad_q, w_query.T, preferred_element_type=jnp.float32)
    grad_normed_one = grad_normed_one + jnp.dot(grad_k, w_key.T, preferred_element_type=jnp.float32)
    grad_normed_one = grad_normed_one + jnp.dot(
        grad_v, w_value.T, preferred_element_type=jnp.float32
    )
    grad_normed_one = lax.psum(grad_normed_one.astype(jnp.bfloat16), "tensor").astype(jnp.float32)
    grad_inner, grad_norm_attn = norm_back(grad_normed_one, inputs, scale_one, norm_attn)
    grad_input = grad_residual + grad_inner
    summed = lax.psum(
        (
            grad_norm_attn,
            grad_w_query,
            grad_w_key,
            grad_w_value,
            grad_w_out,
            grad_norm_ffn,
            grad_router,
            grad_shared_gate,
            grad_shared_up,
            grad_shared_down,
        ),
        "expert",
    )
    return (
        loss,
        final.astype(jnp.bfloat16),
        lax.dynamic_slice_in_dim(grad_input, offset, quarter, 1),
        summed[0],
        summed[1],
        summed[2],
        summed[3],
        summed[4],
        summed[5],
        summed[6],
        summed[7],
        summed[8],
        summed[9],
        grad_expert_gate[None],
        grad_expert_up[None],
        grad_expert_down[None],
    )


def solution(mesh):
    placed = (
        P("expert", None),
        P(),
        P(None, "tensor"),
        P(None, "tensor"),
        P(None, "tensor"),
        P("tensor", None),
        P(),
        P(),
        P(None, "tensor"),
        P(None, "tensor"),
        P("tensor", None),
        P("expert", None, "tensor"),
        P("expert", None, "tensor"),
        P("expert", "tensor", None),
        P("expert"),
        P("expert", None),
        P("expert", None),
        P("expert", "tensor"),
    )
    return jax.shard_map(
        body,
        mesh=mesh,
        in_specs=placed,
        out_specs=(
            P(),
            P("expert", "tensor"),
            P("expert", "tensor"),
            P(),
            P(None, "tensor"),
            P(None, "tensor"),
            P(None, "tensor"),
            P("tensor", None),
            P(),
            P(),
            P(None, "tensor"),
            P(None, "tensor"),
            P("tensor", None),
            P("expert", None, "tensor"),
            P("expert", None, "tensor"),
            P("expert", "tensor", None),
        ),
        check_vma=False,
    )
```

profile of v0, /device:TPU:0, one launch (start us, length us, event | category | flops | bytes accessed | tf_op | source)
XLA Modules:
  0.0 1041.1 jit_solution(12580159714190715911)
XLA Ops:
  14.9 22.3 %while.29 = (s32[]{:T(128)}, bf16[2,3,512,64]{2,3,1,0:T(8,128)(2,1)}, f32[2,3,512]{2,1,0:T(4,128)S(1)}, s32[2]{0:T(128)S(1)}, s32[1024]{0:T(1024)S(1)}, /*index=...) while((s32[]{:T(128)}, ...), condition=%wide.region_4.5_spmd.clone, body=%wide.region_1.4_spmd.sunk.clone | while | flops 423099392 | bytes 25567448 | solution.py:84
  44.9 42.7 %all-reduce.10.cloned.1.call-done = bf16[1024,768]{1,0:T(8,128)(2,1)} async-done(((bf16[1024,768]{1,0:T(8,128)(2,1)}), bf16[1024,768]{1,0:T(8,128)(2,1)}) %all-reduce.10.cloned.1.call-update) | async-done | bytes 1572880 | tf_op jit(solution)/shard_map/psum | solution.py:179
  97.7 7.6 reshape.373
  105.3 13.2 %scatter_custom_fusion = bf16[3073,768]{1,0:T(8,128)(2,1)} fusion(s32[2048]{0:T(1024)S(1)} %bitcast.242, bf16[2048,768]{1,0:T(8,128)(2,1)} %reshape.373, bf16[]{:T(256)} %constant.61.clone.1), kind=kCustom, calls=%fused_computation.70 | custom fusion | bytes 4720640 | tf_op jit(solution)/shard_map/scatter | solution.py:200
  120.8 109.9 %all_to_all.20 = bf16[8,384,768]{2,1,0:T(8,128)(2,1)S(1)} all-to-all(bf16[8,384,768]{2,1,0:T(8,128)(2,1)S(1)} %bitcast.202), channel_id=1, replica_groups=mesh['expert'=8,'tensor'=4] {'expert'}, dimensions={0} | all-to-all | bytes 9437184 | tf_op jit(solution)/shard_map/all_to_all | solution.py:202
  253.3 37.8 %reduce-scatter.6.cloned.1.call-done = bf16[8,384,192]{1,2,0:T(8,128)(2,1)} async-done(((bf16[8,384,768]{1,2,0:T(8,128)(2,1)}), bf16[8,384,192]{1,2,0:T(8,128)(2,1)}) %reduce-scatter.6.cloned.1.call-update) | async-done | bytes 1179664 | tf_op jit(solution)/shard_map/reduce_scatter | solution.py:211
  308.6 14.0 %reduce-scatter.10.cloned.1.call-done = bf16[192,1024]{1,0:T(8,128)(2,1)} async-done(((bf16[768,1024]{1,0:T(8,128)(2,1)}), bf16[192,1024]{1,0:T(8,128)(2,1)}) %reduce-scatter.10.cloned.1.call-update) | async-done | bytes 393232
  330.6 10.1 gather_fusion
  356.7 39.1 %all-reduce.2 = (f32[]{:T(128)}, f32[]{:T(128)}) all-reduce(f32[]{:T(128)S(6)} %div.93, f32[]{:T(128)} %fusion.38), channel_id=1, replica_groups=mesh['expert'=8,'tensor'=4] {'expert','tensor'}, use_global_device_ids=true, to_apply=%region_16.17 | all-reduce | flops 2 | bytes 16 | tf_op jit(solution)/shard_map/psum | solution.py:231
  405.5 12.0 %scatter_custom_fusion.1 = bf16[3073,192]{1,0:T(8,128)(2,1)} fusion(s32[2048]{0:T(1024)S(1)} %bitcast.244, f32[2048,192]{1,0:T(8,128)} %mul.563, f32[2048]{0:T(1024)S(1)} %mul.560, bf16[]{:T(256)} %constant.61.clone.1), kind=kCustom, calls=%fused_computation.92 | custom fusion | flops 786432 | bytes 2761090 | tf_op jit(solution)/shard_map/scatter | solution.py:247
  422.7 33.7 %all_to_all.21 = bf16[8,384,192]{1,2,0:T(8,128)(2,1)S(1)} all-to-all(bf16[8,384,192]{1,2,0:T(8,128)(2,1)} %copy.111), channel_id=1, replica_groups=mesh['expert'=8,'tensor'=4] {'expert'}, dimensions={0} | all-to-all | bytes 2359296 | tf_op jit(solution)/shard_map/all_to_all | solution.py:250
  458.7 34.9 %all-gather.5.cloned.1.call-done = bf16[8,384,768]{1,0,2:T(8,128)(2,1)} async-done(((bf16[8,384,192]{1,0,2:T(8,128)(2,1)}), bf16[8,384,768]{1,0,2:T(8,128)(2,1)}) %all-gather.5.cloned.1.call-update) | async-done | bytes 4718608 | tf_op jit(solution)/shard_map/all_gather | solution.py:251
  497.1 9.7 multiply_convert_fusion.1
  513.9 7.1 copy.113
  526.2 13.5 %psum.116 = bf16[1024,2]{1,0:T(8,128)(2,1)S(1)} all-reduce(bf16[1024,2]{1,0:T(8,128)(2,1)S(1)} %multiply_reduce_fusion.4), channel_id=1, replica_groups=mesh['expert'=8,'tensor'=4] {'tensor'}, use_global_device_ids=true, to_apply=%region_22.23 | all-reduce | flops 2048 | bytes 8192 | tf_op jit(solution)/shard_map/psum | solution.py:292
  540.2 28.7 %reduce-scatter.8.cloned.1.call-done = bf16[8,384,192]{1,0,2:T(8,128)(2,1)} async-done(((bf16[8,384,768]{1,0,2:T(8,128)(2,1)}), bf16[8,384,192]{1,0,2:T(8,128)(2,1)}) %reduce-scatter.8.cloned.1.call-update) | async-done | bytes 1179664 | tf_op jit(solution)/shard_map/reduce_scatter | solution.py:264
  582.3 8.4 all-gather.3.cloned.1.call-done
  610.9 10.1 gather_fusion.1
  654.8 28.3 %all-reduce.12.cloned.1.call-done = bf16[1024,768]{1,0:T(8,128)(2,1)} async-done(((bf16[1024,768]{1,0:T(8,128)(2,1)}), bf16[1024,768]{1,0:T(8,128)(2,1)}) %all-reduce.12.cloned.1.call-update) | async-done | bytes 1572880 | tf_op jit(solution)/shard_map/psum | solution.py:291
  690.5 35.4 %while.30 = (s32[]{:T(128)}, f32[3,1024,64]{1,2,0:T(8,128)}, f32[3,1024,64]{1,2,0:T(8,128)}, f32[2,3,512,64]{2,3,1,0:T(8,128)}, s32[2]{0:T(128)S(1)}, /*index=5*...) while((s32[]{:T(128)}, f32[3,1024,64]{1,2,0:T(8,128)}, ...), condition=%wide.region_27.28_spmd.clone.clone, body=%wide.region_25.27_spmd.clone.sunk.clone | while | flops 1025014784 | bytes 69513584 | solution.py:125
  745.5 7.3 convolution_bitcast_fusion
  760.4 16.3 %all-reduce.14.cloned.1.call-done = bf16[1024,768]{1,0:T(8,128)(2,1)} async-done(((bf16[1024,768]{1,0:T(8,128)(2,1)}), bf16[1024,768]{1,0:T(8,128)(2,1)}) %all-reduce.14.cloned.1.call-update) | async-done | bytes 1572880 | tf_op jit(solution)/shard_map/psum | solution.py:319
  783.1 39.8 %all-reduce.3 = (f32[768]{0:T(1024)}, f32[768]{0:T(1024)}, f32[768,8]{0,1:T(8,128)}) all-reduce(f32[768]{0:T(1024)S(1)} %get-tuple-element.241, f32[768]{0:T(1024)S(1)} %get-tuple-element.239, f32[768,8]{0,1:T(8,128)S(1)} %fusion.66), channel_id=1, replica_groups=mesh['expert'=8,'tensor'=4] {'expert'}, use_global_device_ids=true, to_apply=%region_31.32 | all-reduce | flops 7680 | bytes 61440 | tf_op jit(solution)/shard_map/psum | solution.py:322
  822.9 199.8 %all-reduce.16.cloned.1.call-done = (f32[768,192]{0,1:T(8,128)}, f32[768,192]{0,1:T(8,128)}, f32[768,192]{0,1:T(8,128)}, f32[192,768]{1,0:T(8,128)}, f32[768,512...) async-done(((f32[768,192]{0,1:T(8,128)}, f32[768,192]{0,1:T(8,128)}, f32[768,192]{0,1:T(8,128)}, f32[192,768]{1,0:T(8,128)}, f32[768,512]{1,0:T(8,128)}, ...) | async-done | bytes 7077904 | tf_op jit(solution)/shard_map/psum | solution.py:322
  (367 shorter events, 289.7 us)
Async XLA Ops:
  7.2 233.2 %copy-start = (bf16[1,512,768]{2,1,0:T(8,128)(2,1)S(1)}, bf16[1,512,768]{2,1,0:T(8,128)(2,1)}, u32[]{:S(2)}) copy-start(bf16[1,512,768]{2,1,0:T(8,128)(2,1)} %param.35) | copy-start | bytes 2359300
  7.2 80.4 %all-reduce.10.cloned.1.call-start = ((), (), s32[]{:S(2)}) async-start(), calls=%async_computation.7 | async-start | bytes 3145728 | tf_op jit(solution)/shard_map/psum | solution.py:179
  37.2 54.1 %copy-start.15 = (bf16[3,1024,64]{1,2,0:T(8,128)(2,1)}, bf16[3,1024,64]{1,2,0:T(8,128)(2,1)S(1)}, u32[]{:S(2)}) copy-start(bf16[3,1024,64]{1,2,0:T(8,128)(2,1)S(1)} %get-tuple-element.603) | copy-start | bytes 1179652
  37.2 54.1 %copy-start.56 = (f32[2,3,512]{2,1,0:T(4,128)}, f32[2,3,512]{2,1,0:T(4,128)S(1)}, u32[]{:S(2)}) copy-start(f32[2,3,512]{2,1,0:T(4,128)S(1)} %get-tuple-element.119) | copy-start | bytes 36868
  41.9 249.2 %reduce-scatter.6.cloned.1.call-start = ((), (), s32[]{:S(2)}) async-start(), calls=%async_computation.8 | async-start | bytes 5898240 | tf_op jit(solution)/shard_map/reduce_scatter | solution.py:211
  44.9 46.4 %copy-start.66 = (f32[768]{0:T(1024)S(1)}, f32[768]{0:T(1024)}, u32[]{:S(2)}) copy-start(f32[768]{0:T(1024)} %param.28) | copy-start | bytes 9220
  120.8 109.9 %copy-start.71 = (bf16[1,768,512]{2,1,0:T(8,128)(2,1)S(1)}, bf16[1,768,512]{2,1,0:T(8,128)(2,1)}, u32[]{:S(2)}) copy-start(bf16[1,768,512]{2,1,0:T(8,128)(2,1)} %param.33) | copy-start | bytes 2359300
  244.7 77.9 %reduce-scatter.10.cloned.1.call-start = ((), (), s32[]{:S(2)}) async-start(), calls=%async_computation.14 | async-start | bytes 1966080
  253.3 44.7 %copy-start.53 = (bf16[1024,192]{0,1:T(8,128)(2,1)S(1)}, bf16[1024,192]{0,1:T(8,128)(2,1)}, u32[]{:S(2)}) copy-start(bf16[1024,192]{0,1:T(8,128)(2,1)} %param.39) | copy-start | bytes 1179652
  253.3 46.9 %copy-start.64 = (bf16[768,8]{0,1:T(8,128)(2,1)S(1)}, bf16[768,8]{0,1:T(8,128)(2,1)}, u32[]{:S(2)}) copy-start(bf16[768,8]{0,1:T(8,128)(2,1)} %param.29) | copy-start | bytes 36868
  291.1 34.2 %all-to-all-start.1 = ((bf16[8,384,192]{1,2,0:T(8,128)(2,1)}), bf16[8,384,192]{1,2,0:T(8,128)(2,1)}, u32[]{:S(2)}, u32[]{:S(2)}) async-start(bf16[8,384,192]{1,2,0:T(8,128)(2,1)} %reduce-scatter.6.cloned.1.call-done), calls=%async_computation.2 | async-start | bytes 2359296 | tf_op jit(solution)/shard_map/all_to_all | solution.py:218
  296.6 196.9 %all-gather.5.cloned.1.call-start = ((), (), s32[]{:S(2)}) async-start(), calls=%async_computation.10 | async-start | bytes 5898240 | tf_op jit(solution)/shard_map/all_gather | solution.py:251
  307.4 23.2 %copy-start.58 = (f32[1024]{0:T(1024)}, f32[1024]{0:T(1024)S(1)}, u32[]{:S(2)}) copy-start(f32[1024]{0:T(1024)S(1)} %fusion.65) | copy-start | bytes 12292
  458.2 110.8 %reduce-scatter.8.cloned.1.call-start = ((), (), s32[]{:S(2)}) async-start(), calls=%async_computation.11 | async-start | bytes 5898240 | tf_op jit(solution)/shard_map/reduce_scatter | solution.py:264
  520.9 69.8 %all-gather.3.cloned.1.call-start = ((), (), s32[]{:S(2)}) async-start(), calls=%async_computation.9 | async-start | bytes 1966080 | tf_op jit(solution)/shard_map/all_gather | solution.py:236
  571.4 34.2 %all-to-all-start.3 = ((bf16[8,384,192]{1,2,0:T(8,128)(2,1)}), bf16[8,384,192]{1,2,0:T(8,128)(2,1)}, u32[]{:S(2)}, u32[]{:S(2)}) async-start(bf16[8,384,192]{1,2,0:T(8,128)(2,1)} %copy.114), calls=%async_computation.5 | async-start | bytes 2359296 | tf_op jit(solution)/shard_map/all_to_all | solution.py:270
  576.9 106.2 %all-reduce.12.cloned.1.call-start = ((), (), s32[]{:S(2)}) async-start(), calls=%async_computation.12 | async-start | bytes 3145728 | tf_op jit(solution)/shard_map/psum | solution.py:291
  582.2 100.9 %copy-start.26 = (f32[1024,1,8]{2,1,0:T(1,128)}, f32[1024,1,8]{2,1,0:T(1,128)S(1)}, u32[]{:S(2)}) copy-start(f32[1024,1,8]{2,1,0:T(1,128)S(1)} %fusion.44) | copy-start | bytes 98308
  641.8 134.9 %all-reduce.14.cloned.1.call-start = ((), (), s32[]{:S(2)}) async-start(), calls=%async_computation.13 | async-start | bytes 3145728 | tf_op jit(solution)/shard_map/psum | solution.py:319
  652.5 30.6 %copy-start.61 = (f32[1024]{0:T(1024)S(1)}, f32[1024]{0:T(1024)}, u32[]{:S(2)}) copy-start(f32[1024]{0:T(1024)} %copy-done.60) | copy-start | bytes 12292
  652.5 30.6 %copy-start.65 = (bf16[768,8]{0,1:T(8,128)(2,1)S(1)}, bf16[768,8]{0,1:T(8,128)(2,1)}, u32[]{:S(2)}) copy-start(bf16[768,8]{0,1:T(8,128)(2,1)} %param.29) | copy-start | bytes 36868
  652.5 30.6 %copy-start.67 = (f32[768]{0:T(1024)S(1)}, f32[768]{0:T(1024)}, u32[]{:S(2)}) copy-start(f32[768]{0:T(1024)} %param.28) | copy-start | bytes 9220
  733.6 289.1 %all-reduce.16.cloned.1.call-start = ((), (), s32[]{:S(2)}) async-start(), calls=%async_computation.15 | async-start | bytes 14155776 | tf_op jit(solution)/shard_map/psum | solution.py:322
  756.7 20.0 %copy-start.69 = (f32[768]{0:T(1024)S(1)}, f32[768]{0:T(1024)}, u32[]{:S(2)}) copy-start(f32[768]{0:T(1024)} %param.23) | copy-start | bytes 9220
  (85 other events, 313.9 us)
Sparse Core Ops, SparseCore 0:
  42.0 45.5 all-reduce.9
  244.8 46.2 reduce-scatter.5
  294.4 28.1 reduce-scatter.9
  458.3 35.2 all-gather.4
  521.1 47.8 reduce-scatter.7
  571.0 19.6 all-gather.2
  641.9 41.1 all-reduce.11
  733.8 42.9 all-reduce.13
  784.1 238.6 all-reduce.15
where the time goes:
time: 1050 us; the launch traced here: 1040 us
  waiting for transfers between devices  417 us (40%)
  blocking collectives  236 us (22%)
  local copies, waits for them, and re-layouts  140 us (13%)
  matrix products  136 us (13%)
  other arithmetic  71.6 us (7%)
  between operations  19 us (2%)
  starting transfers between devices  12.9 us (1%)
    psum x1, waiting for transfers between devices, body(): lax.psum((grad_norm_attn, grad_w_query, grad_w_key, grad_w_value, grad_w_...  200 us
    all_to_all x1, blocking collectives, body(): lax.all_to_all(outgoing, 'expert', split_axis=0, concat_axis=0, tiled=True)  110 us
    psum x1, waiting for transfers between devices, body(): lax.psum(jnp.dot(mixed_low, w_out, preferred_element_type=jnp.float32).as...  42.7 us
    psum x1, blocking collectives, body(): lax.psum((grad_norm_attn, grad_w_query, grad_w_key, grad_w_value, grad_w_...  39.8 us
    psum x1, blocking collectives, body(): lax.psum((jnp.sum(valid[:, None] * error * error), jnp.sum(valid) / membe...  39.1 us
    reduce_scatter x1, waiting for transfers between devices, body(): lax.psum_scatter(expert_part.astype(jnp.bfloat16), 'tensor', scatter_dime...  37.8 us
    all_gather x1, waiting for transfers between devices, body(): lax.all_gather(grad_arrived, 'tensor', axis=2, tiled=True)  34.9 us
    all_to_all x1, blocking collectives, body(): lax.all_to_all(grad_buffer, 'expert', split_axis=0, concat_axis=0, tiled=...  33.7 us
  transfers between devices with their start and end apart: 11, of which 11 were waited for; matrix products, arithmetic and copies ran while one was open for 8% of the time, Pallas kernels for 0%

commit v1 on v0

v1 whole, which is shorter than its diff:
```python
import jax
import jax.numpy as jnp
from jax import lax
from jax.sharding import PartitionSpec as P

HD = 64


eps_norm = 1e-06


def rope_tables(length, head_dim):
    half = head_dim // 2
    freqs = 10000.0 ** (-2.0 * jnp.arange(half, dtype=jnp.float32) / head_dim)
    angles = jnp.arange(length, dtype=jnp.float32)[:, None] * freqs[None, :]
    return (jnp.cos(angles), jnp.sin(angles))


def rotate(vec, cosine, sine):
    half = vec.shape[-1] // 2
    first = vec[..., :half]
    second = vec[..., half:]
    return jnp.concatenate(
        [first * cosine - second * sine, second * cosine + first * sine], axis=-1
    )


def rotate_back(grad, cosine, sine):
    half = grad.shape[-1] // 2
    first = grad[..., :half]
    second = grad[..., half:]
    return jnp.concatenate(
        [first * cosine + second * sine, second * cosine - first * sine], axis=-1
    )


def silu_slope(value):
    sigma = jax.nn.sigmoid(value)
    return sigma * (1.0 + value * (1.0 - sigma))


def norm_back(grad, value, scale, gain):
    scaled = grad * gain
    inner = jnp.mean(scaled * value, axis=-1, keepdims=True)
    return (
        scale * scaled - value * scale * scale * scale * inner,
        jnp.sum(grad * value * scale, axis=0),
    )


def split_heads(flat, heads):
    return flat.reshape(flat.shape[0], heads, -1).transpose(1, 0, 2)


def merge_heads(stacked):
    return stacked.transpose(1, 0, 2).reshape(stacked.shape[1], -1)


def block_scores(q_block, keys, segment, start, block):
    length = keys.shape[1]
    scale = keys.shape[2] ** (-0.5)
    seg_block = lax.dynamic_slice_in_dim(segment, start, block, 0)
    places = jnp.arange(length)
    rows_at = start + jnp.arange(block)
    allowed = (seg_block[:, None] == segment[None, :]) & (places[None, :] <= rows_at[:, None])
    scores = jnp.einsum("hqd,hkd->hqk", q_block, keys, preferred_element_type=jnp.float32) * scale
    return (jnp.where(allowed[None], scores, -1e30), allowed)


def attend_forward(query, keys, values, segment, block):
    heads, length, width = query.shape

    def one_block(start):
        q_block = lax.dynamic_slice_in_dim(query, start, block, 1)
        scores, allowed = block_scores(q_block, keys, segment, start, block)
        top = jnp.max(scores, axis=-1, keepdims=True)
        expo = jnp.exp(scores - top)
        total = jnp.sum(expo, axis=-1, keepdims=True)
        prob = (expo / total).astype(jnp.bfloat16)
        mixed = jnp.einsum("hqk,hkd->hqd", prob, values, preferred_element_type=jnp.float32)
        return (mixed, (top + jnp.log(total))[..., 0])

    starts = jnp.arange(length // block) * block
    mixed, summary = lax.map(one_block, starts)
    mixed = mixed.transpose(1, 0, 2, 3).reshape(heads, length, width)
    summary = summary.transpose(1, 0, 2).reshape(heads, length)
    return (mixed, summary)


def attend_backward(query, keys, values, segment, summary, grad_mixed, block):
    heads, length, width = query.shape
    scale = width ** (-0.5)

    def one_block(carry, start):
        grad_keys, grad_values = carry
        q_block = lax.dynamic_slice_in_dim(query, start, block, 1)
        scores, allowed = block_scores(q_block, keys, segment, start, block)
        sum_block = lax.dynamic_slice_in_dim(summary, start, block, 1)
        prob = jnp.where(allowed[None], jnp.exp(scores - sum_block[..., None]), 0.0)
        grad_block = lax.dynamic_slice_in_dim(grad_mixed, start, block, 1)
        grad_prob = jnp.einsum(
            "hqd,hkd->hqk", grad_block, values, preferred_element_type=jnp.float32
        )
        inner = jnp.sum(prob * grad_prob, axis=-1, keepdims=True)
        grad_scores = (prob * (grad_prob - inner)).astype(jnp.bfloat16)
        grad_q = (
            jnp.einsum("hqk,hkd->hqd", grad_scores, keys, preferred_element_type=jnp.float32)
            * scale
        )
        grad_keys = (
            grad_keys
            + jnp.einsum("hqk,hqd->hkd", grad_scores, q_block, preferred_element_type=jnp.float32)
            * scale
        )
        grad_values = grad_values + jnp.einsum(
            "hqk,hqd->hkd",
            prob.astype(jnp.bfloat16),
            grad_block,
            preferred_element_type=jnp.float32,
        )
        return ((grad_keys, grad_values), grad_q)

    starts = jnp.arange(length // block) * block
    zeros = jnp.zeros((heads, length, width), jnp.float32)
    (grad_keys, grad_values), grad_q = lax.scan(one_block, (zeros, zeros), starts)
    grad_q = grad_q.transpose(1, 0, 2, 3).reshape(heads, length, width)
    return (grad_q, grad_keys, grad_values)


def body(
    hidden_in,
    norm_attn,
    w_query,
    w_key,
    w_value,
    w_out,
    norm_ffn,
    w_router,
    shared_gate,
    shared_up,
    shared_down,
    expert_gate,
    expert_up,
    expert_down,
    segment,
    routes,
    slots,
    teacher,
):
    length, width = hidden_in.shape
    groups = lax.axis_size("expert")
    members = lax.axis_size("tensor")
    me = lax.axis_index("tensor")
    quarter = width // members
    experts = w_router.shape[1]
    capacity = 3 * length // groups
    share = capacity // members
    rows = groups * share
    tokens = length * groups
    local_heads = w_query.shape[1] // HD
    block = min(512, length)
    f32, bf16 = jnp.float32, jnp.bfloat16

    def mm(a, b):
        return jnp.dot(a, b, preferred_element_type=f32)

    gate_all = lax.all_gather(expert_gate[0], "tensor", axis=0)
    up_all = lax.all_gather(expert_up[0], "tensor", axis=0)
    down_all = lax.all_gather(expert_down[0], "tensor", axis=0)
    out_all = lax.all_gather(w_out, "tensor", axis=0)

    inputs = hidden_in.astype(f32)
    scale_one = lax.rsqrt(jnp.mean(inputs * inputs, axis=-1, keepdims=True) + eps_norm)
    normed_one = (inputs * scale_one * norm_attn).astype(bf16)
    cosine, sine = rope_tables(length, HD)
    query = rotate(split_heads(mm(normed_one, w_query), local_heads), cosine, sine).astype(bf16)
    keys = rotate(split_heads(mm(normed_one, w_key), local_heads), cosine, sine).astype(bf16)
    values = split_heads(mm(normed_one, w_value), local_heads).astype(bf16)
    mixed, summary = attend_forward(query, keys, values, segment, block)
    mixed_low = merge_heads(mixed).astype(bf16)
    mixed_all = lax.all_gather(mixed_low, "tensor", axis=0)
    attention = jnp.einsum("mth,mhd->td", mixed_all, out_all, preferred_element_type=f32)
    residual = inputs + attention
    scale_two = lax.rsqrt(jnp.mean(residual * residual, axis=-1, keepdims=True) + eps_norm)
    normed_two = (residual * scale_two * norm_ffn).astype(bf16)
    logits = mm(normed_two, w_router)
    onehot = (routes[:, :, None] == jnp.arange(experts, dtype=jnp.int32)[None, None, :]).astype(f32)
    chosen = jnp.sum(logits[:, None, :] * onehot, axis=2)
    gates = jax.nn.softmax(chosen, axis=1)
    mine = (slots < capacity) & (slots // share == me)
    place = jnp.where(mine, routes * share + slots - me * share, -1)
    columns = jnp.arange(rows, dtype=jnp.int32)[None, :]
    pick = [(place[:, k][:, None] == columns).astype(bf16) for k in range(2)]
    outgoing = mm((pick[0] + pick[1]).T, normed_two).astype(bf16).reshape(groups, share, width)
    arrived = lax.all_to_all(outgoing, "expert", split_axis=0, concat_axis=0, tiled=True)
    side_pre = mm(normed_two, shared_gate)
    side_lin = mm(normed_two, shared_up)
    side_hidden = (jax.nn.silu(side_pre) * side_lin).astype(bf16)
    side_part = mm(side_hidden, shared_down)
    rows_in = arrived.reshape(rows, width)
    pre = [mm(rows_in, gate_all[m]) for m in range(members)]
    lin = [mm(rows_in, up_all[m]) for m in range(members)]
    hid = [(jax.nn.silu(p) * u).astype(bf16) for p, u in zip(pre, lin)]
    made = sum(mm(hid[m], down_all[m]) for m in range(members))
    returned = lax.all_to_all(
        made.astype(bf16).reshape(groups, share, width),
        "expert",
        split_axis=0,
        concat_axis=0,
        tiled=True,
    ).reshape(rows, width)
    fetched = [mm(p, returned) for p in pick]
    mixture = gates[:, 0:1] * fetched[0] + gates[:, 1:2] * fetched[1]
    own = lax.dynamic_slice_in_dim
    part_sum = lax.psum_scatter(
        (side_part + mixture).astype(bf16), "tensor", scatter_dimension=1, tiled=True
    ).astype(f32)
    final = own(residual, me * quarter, quarter, 1) + part_sum
    valid = (segment != 0).astype(f32)
    error = (final - teacher.astype(f32)) * valid[:, None]
    grad_full = lax.all_gather(error.astype(bf16), "tensor", axis=1, tiled=True)
    grad_wide = grad_full.astype(f32)
    gate_part = jnp.concatenate(
        [jnp.sum(grad_wide * f, axis=1, keepdims=True) for f in fetched], axis=1
    )
    pair_grad = [(gates[:, k : k + 1] * grad_wide).astype(bf16) for k in range(2)]
    grad_out_rows = (mm(pick[0].T, pair_grad[0]) + mm(pick[1].T, pair_grad[1])).astype(bf16)
    grad_arrived = lax.all_to_all(
        grad_out_rows.reshape(groups, share, width), "expert", split_axis=0, concat_axis=0, tiled=True
    ).reshape(rows, width)
    grad_side_hidden = mm(grad_full, shared_down.T)
    grad_shared_down = mm(side_hidden.T, grad_full)
    side_pre_grad = (grad_side_hidden * side_lin * silu_slope(side_pre)).astype(bf16)
    side_lin_grad = (grad_side_hidden * jax.nn.silu(side_pre)).astype(bf16)
    grad_shared_gate = mm(normed_two.T, side_pre_grad)
    grad_shared_up = mm(normed_two.T, side_lin_grad)
    grad_normed = mm(side_pre_grad, shared_gate.T) + mm(side_lin_grad, shared_up.T)

    grad_hid = [mm(grad_arrived, down_all[m].T) for m in range(members)]
    pre_grad = [
        (g * u * silu_slope(p)).astype(bf16) for g, u, p in zip(grad_hid, lin, pre)
    ]
    lin_grad = [(g * jax.nn.silu(p)).astype(bf16) for g, p in zip(grad_hid, pre)]
    grad_rows = sum(
        mm(pre_grad[m], gate_all[m].T) + mm(lin_grad[m], up_all[m].T) for m in range(members)
    )
    grad_back = lax.all_to_all(
        grad_rows.astype(bf16).reshape(groups, share, width),
        "expert",
        split_axis=0,
        concat_axis=0,
        tiled=True,
    ).reshape(rows, width)

    def reduced(parts):
        return lax.psum_scatter(jnp.stack(parts), "tensor", scatter_dimension=0)

    grad_expert_down = reduced([mm(h.T, grad_arrived).astype(bf16) for h in hid])
    grad_expert_gate = reduced([mm(rows_in.T, g).astype(bf16) for g in pre_grad])
    grad_expert_up = reduced([mm(rows_in.T, g).astype(bf16) for g in lin_grad])

    grad_normed = grad_normed + mm(pick[0] + pick[1], grad_back)
    grad_chosen = gates * (gate_part - jnp.sum(gates * gate_part, axis=1, keepdims=True))
    grad_logits = jnp.sum(grad_chosen[:, :, None] * onehot, axis=1).astype(bf16)
    grad_router = mm(normed_two.T, grad_logits)
    grad_normed = grad_normed + mm(grad_logits, w_router.T)
    grad_normed = lax.psum(grad_normed.astype(bf16), "tensor").astype(f32)
    grad_through, grad_norm_ffn = norm_back(grad_normed, residual, scale_two, norm_ffn)
    grad_residual = grad_wide + grad_through
    grad_attention = grad_residual.astype(bf16)
    grad_w_out = mm(mixed_low.T, grad_attention)
    grad_mixed = split_heads(mm(grad_attention, w_out.T), local_heads).astype(bf16)
    grad_q, grad_k, grad_v = attend_backward(
        query, keys, values, segment, summary, grad_mixed, block
    )
    grad_q = merge_heads(rotate_back(grad_q, cosine, sine)).astype(bf16)
    grad_k = merge_heads(rotate_back(grad_k, cosine, sine)).astype(bf16)
    grad_v = merge_heads(grad_v).astype(bf16)
    grad_w_query = mm(normed_one.T, grad_q)
    grad_w_key = mm(normed_one.T, grad_k)
    grad_w_value = mm(normed_one.T, grad_v)
    grad_normed_one = mm(grad_q, w_query.T) + mm(grad_k, w_key.T) + mm(grad_v, w_value.T)
    grad_normed_one = lax.psum(grad_normed_one.astype(bf16), "tensor").astype(f32)
    grad_inner, grad_norm_attn = norm_back(grad_normed_one, inputs, scale_one, norm_attn)
    grad_input = grad_residual + grad_inner
    early = lax.psum(
        tuple(g.astype(bf16) for g in (grad_shared_gate, grad_shared_up, grad_shared_down)), "expert"
    )
    late = lax.psum(
        tuple(g.astype(bf16) for g in (grad_w_query, grad_w_key, grad_w_value, grad_w_out)), "expert"
    )
    square_sum, count, grad_router, grad_norm_ffn, grad_norm_attn = lax.psum(
        (
            jnp.sum(error * error),
            jnp.sum(valid) / members,
            grad_router,
            grad_norm_ffn / members,
            grad_norm_attn / members,
        ),
        ("expert", "tensor"),
    )
    factor = 2.0 * tokens / count

    def scaled(value):
        return value.astype(f32) * factor

    return (
        square_sum / (count * width),
        final.astype(bf16),
        scaled(own(grad_input, me * quarter, quarter, 1)),
        scaled(grad_norm_attn),
        *(scaled(g) for g in late),
        scaled(grad_norm_ffn),
        scaled(grad_router),
        *(scaled(g) for g in early),
        scaled(grad_expert_gate)[None],
        scaled(grad_expert_up)[None],
        scaled(grad_expert_down)[None],
    )


def solution(mesh):
    placed = (
        P("expert", None),
        P(),
        P(None, "tensor"),
        P(None, "tensor"),
        P(None, "tensor"),
        P("tensor", None),
        P(),
        P(),
        P(None, "tensor"),
        P(None, "tensor"),
        P("tensor", None),
        P("expert", None, "tensor"),
        P("expert", None, "tensor"),
        P("expert", "tensor", None),
        P("expert"),
        P("expert", None),
        P("expert", None),
        P("expert", "tensor"),
    )
    return jax.shard_map(
        body,
        mesh=mesh,
        in_specs=placed,
        out_specs=(
            P(),
            P("expert", "tensor"),
            P("expert", "tensor"),
            P(),
            P(None, "tensor"),
            P(None, "tensor"),
            P(None, "tensor"),
            P("tensor", None),
            P(),
            P(),
            P(None, "tensor"),
            P(None, "tensor"),
            P("tensor", None),
            P("expert", None, "tensor"),
            P("expert", None, "tensor"),
            P("expert", "tensor", None),
        ),
        check_vma=False,
    )
```

time: 1050 us -> 786 us (0.75)
  blocking collectives: 236 us -> 110 us
  local copies, waits for them, and re-layouts: 140 us -> 29.6 us
  waiting for transfers between devices: 417 us -> 386 us
  matrix products: 136 us -> 150 us
  other arithmetic: 71.6 us -> 60.9 us
    psum x4 -> x3, waiting for transfers between devices: 287 us -> 186 us  [the longest x1 145 us: body(): lax.psum(tuple((g.astype(bf16) for g in (grad_w_query, grad_w_key, grad_w...]
    all_to_all x1, blocking collectives: 110 us -> 34.9 us  [body(): lax.all_to_all(outgoing, 'expert', split_axis=0, concat_axis=0, tiled=True)]
    psum x3 -> x1, blocking collectives: 92.4 us -> 40.2 us  [body(): lax.psum((jnp.sum(error * error), jnp.sum(valid) / members, grad_router,...]
    all_to_all x2, waiting for transfers between devices: 6.12 us -> 37.1 us  [the longest x1 21.1 us: body(): lax.all_to_all(made.astype(bf16).reshape(groups, share, width), 'expert',...]
    all_gather x2 -> x6, waiting for transfers between devices: 43.3 us -> 69.9 us  [the longest x1 22.1 us: body(): down_all = lax.all_gather(expert_down[0], 'tensor', axis=0)]
    reduce_scatter x2 -> x4, waiting for transfers between devices: 66.6 us -> 91.3 us  [the longest x3 64.9 us: reduced(): return lax.psum_scatter(jnp.stack(parts), 'tensor', scatter_dimension=0)]
    mul x1 -> x15, other arithmetic: 0.48 us -> 22.5 us  [the longest x14 22.5 us: scaled(): return value.astype(f32) * factor]
    gather x2 -> x0, local copies, waits for them, and re-layouts: 20.2 us -> none  [the longest x1 10.1 us: body(): fetched = lookup[target].reshape(length, 2, quarter).astype(jnp.float32)]
  transfers between devices with their start and end apart: 11 -> 15, of which waited for: 11 -> 12; matrix products, arithmetic and copies ran while one was open for 8% -> 16% of each run, Pallas kernels for 0% -> 0%
where the time goes in v1:
time: 786 us; the launch traced here: 776 us
  waiting for transfers between devices  386 us (49%)
  matrix products  150 us (19%)
  blocking collectives  110 us (14%)
  other arithmetic  60.9 us (8%)
  local copies, waits for them, and re-layouts  29.6 us (4%)
  between operations  19.2 us (2%)
  starting transfers between devices  11.6 us (1%)
  loops' own time  8.04 us (1%)
    psum x1, waiting for transfers between devices, body(): lax.psum(tuple((g.astype(bf16) for g in (grad_w_query, grad_w_key, grad_w...  145 us
    dot_general x65, matrix products, mm(): return jnp.dot(a, b, preferred_element_type=f32)  113 us
    reduce_scatter x3, waiting for transfers between devices, reduced(): return lax.psum_scatter(jnp.stack(parts), 'tensor', scatter_dimension=0)  64.9 us
    psum x1, blocking collectives, body(): lax.psum((jnp.sum(error * error), jnp.sum(valid) / members, grad_router,...  40.2 us
    psum x1, waiting for transfers between devices, body(): grad_normed = lax.psum(grad_normed.astype(bf16), 'tensor').astype(f32)  36 us
    all_to_all x1, blocking collectives, body(): lax.all_to_all(outgoing, 'expert', split_axis=0, concat_axis=0, tiled=True)  34.9 us
    all_to_all x1, blocking collectives, body(): lax.all_to_all(grad_out_rows.reshape(groups, share, width), 'expert', spl...  34.9 us
    reduce_scatter x1, waiting for transfers between devices, body(): lax.psum_scatter((side_part + mixture).astype(bf16), 'tensor', scatter_di...  26.4 us
  transfers between devices with their start and end apart: 15, of which 12 were waited for; matrix products, arithmetic and copies ran while one was open for 16% of the time, Pallas kernels for 0%

profile of v1, /device:TPU:0, one launch (start us, length us, event | category | flops | bytes accessed | tf_op | source)
XLA Modules:
  0.0 775.7 jit_solution(709133124578278240)
XLA Ops:
  14.8 24.0 %while.29 = (s32[]{:T(128)}, bf16[2,3,512,64]{2,3,1,0:T(8,128)(2,1)S(1)}, f32[2,3,512]{2,1,0:T(4,128)}, s32[2]{0:T(128)S(1)}, s32[1024]{0:T(1024)S(1)}, /*index=...) while((s32[]{:T(128)}, ...), condition=%wide.region_4.5_spmd.clone, body=%wide.region_1.4_spmd.sunk.clone | while | flops 423099392 | bytes 22520024 | solution.py:84
  41.7 20.5 %all-gather.8.cloned.1.call-done = bf16[4,1024,192]{1,2,0:T(8,128)(2,1)} async-done(((bf16[1,1024,192]{1,2,0:T(8,128)(2,1)}), bf16[4,1024,192]{1,2,0:T(8,128)(2,1)}) %all-gather.8.cloned.1.call-update) | async-done | bytes 1572880 | tf_op jit(solution)/shard_map/all_gather | solution.py:181
  69.3 34.9 %all_to_all.20 = bf16[8,96,768]{2,1,0:T(8,128)(2,1)} all-to-all(bf16[8,96,768]{2,1,0:T(8,128)(2,1)S(1)} %bitcast.328), channel_id=1, replica_groups=mesh['expert'=8,'tensor'=4] {'expert'}, dimensions={0} | all-to-all | bytes 2359296 | tf_op jit(solution)/shard_map/all_to_all | solution.py:195
  114.9 7.4 all-gather.12.cloned.1.call-done
  122.3 4.1 multiply_convert_fusion.17
  130.2 22.1 %all-gather.14.cloned.1.call-done = bf16[4,512,768]{2,1,0:T(8,128)(2,1)} async-done(((bf16[1,512,768]{2,1,0:T(8,128)(2,1)}), bf16[4,512,768]{2,1,0:T(8,128)(2,1)}) %all-gather.14.cloned.1.call-update) | async-done | bytes 3145744 | tf_op jit(solution)/shard_map/all_gather | solution.py:169
  166.5 5.6 all-to-all-start.1
  180.1 21.1 %all-to-all-done.1 = bf16[8,96,768]{2,1,0:T(8,128)(2,1)} async-done(((bf16[8,96,768]{2,1,0:T(8,128)(2,1)}), bf16[8,96,768]{2,1,0:T(8,128)(2,1)}, u32[]{:S(2)}, u32[]{:S(2)}) %all-to-all-start.1) | async-done | bytes 1179680 | tf_op jit(solution)/shard_map/all_to_all | solution.py:205
  204.2 3.9 fusion.45
  212.1 26.4 %reduce-scatter.5.cloned.1.call-done = bf16[1024,192]{0,1:T(8,128)(2,1)} async-done(((bf16[1024,768]{0,1:T(8,128)(2,1)}), bf16[1024,192]{0,1:T(8,128)(2,1)}) %reduce-scatter.5.cloned.1.call-update) | async-done | bytes 393232 | tf_op jit(solution)/shard_map/reduce_scatter | solution.py:215
  241.5 19.8 %all-gather.16.cloned.1.call-done = bf16[1024,768]{0,1:T(8,128)(2,1)} async-done(((bf16[1024,192]{0,1:T(8,128)(2,1)}), bf16[1024,768]{0,1:T(8,128)(2,1)}) %all-gather.16.cloned.1.call-update) | async-done | bytes 1572880 | tf_op jit(solution)/shard_map/all_gather | solution.py:221
  266.2 34.9 %all_to_all.21 = bf16[8,96,768]{2,1,0:T(8,128)(2,1)S(1)} all-to-all(bf16[8,96,768]{2,1,0:T(8,128)(2,1)S(1)} %bitcast.327), channel_id=1, replica_groups=mesh['expert'=8,'tensor'=4] {'expert'}, dimensions={0} | all-to-all | bytes 2359296 | tf_op jit(solution)/shard_map/all_to_all | solution.py:228
  318.3 4.2 all-to-all-start.3
  334.4 16.0 %all-to-all-done.3 = bf16[8,96,768]{2,1,0:T(8,128)(2,1)} async-done(((bf16[8,96,768]{2,1,0:T(8,128)(2,1)}), bf16[8,96,768]{2,1,0:T(8,128)(2,1)}, u32[]{:S(2)}, u32[]{:S(2)}) %all-to-all-start.3) | async-done | bytes 1179680 | tf_op jit(solution)/shard_map/all_to_all | solution.py:247
  360.5 36.0 %all-reduce.6.cloned.1.call-done = bf16[1024,768]{0,1:T(8,128)(2,1)} async-done(((bf16[1024,768]{0,1:T(8,128)(2,1)}), bf16[1024,768]{0,1:T(8,128)(2,1)}) %all-reduce.6.cloned.1.call-update) | async-done | bytes 1572880 | tf_op jit(solution)/shard_map/psum | solution.py:267
  405.7 33.5 %while.30 = (s32[]{:T(128)}, f32[3,1024,64]{1,2,0:T(8,128)S(1)}, f32[3,1024,64]{1,2,0:T(8,128)S(1)}, f32[2,3,512,64]{2,3,1,0:T(8,128)}, s32[2]{0:T(128)S(1)}, /*...) while((s32[]{:T(128)}, f32[3,1024,64]{1,2,0:T(8,128)S(1)}, ...), condition=%wide.region_22.23_spmd.clone.clone, body=%wide.region_20.22_spmd.clone.sunk.clone | while | flops 1025014784 | bytes 60076292 | solution.py:125
  411.9 4.4 multiply_reduce_fusion.6
  428.7 4.4 multiply_reduce_fusion.6
  483.4 4.6 all-reduce.8.cloned.1.call-done
  488.0 5.2 fusion.38
  493.2 40.2 %all-reduce = (f32[]{:T(128)}, f32[]{:T(128)}, f32[768]{0:T(1024)S(1)}, f32[768]{0:T(1024)S(1)}, f32[768,8]{0,1:T(8,128)S(1)}) all-reduce(f32[]{:T(128)} %get-tuple-element.222, f32[]{:T(128)S(6)} %div.128, f32[768]{0:T(1024)S(1)} %broadcast_multiply_fusion.4, ...), channel_id=1, replica_groups=mesh['expert'=8,'tensor'=4] {'expert','tensor'}, use_global_device_ids=true, to_apply=%region_11.12 | all-reduce | flops 7682 | bytes 61456 | tf_op jit(solution)/shard_map/psum | solution.py:292
  542.6 26.7 %reduce-scatter.11.cloned.1.call-done = bf16[1,512,768]{2,1,0:T(8,128)(2,1)} async-done(((bf16[4,512,768]{2,1,0:T(8,128)(2,1)}), bf16[1,512,768]{2,1,0:T(8,128)(2,1)}) %reduce-scatter.11.cloned.1.call-update) | async-done | bytes 786448 | tf_op jit(solution)/shard_map/reduce_scatter | solution.py:256
  571.7 38.2 %reduce-scatter.7.cloned.1.call-done = bf16[1,768,512]{2,1,0:T(8,128)(2,1)} async-done(((bf16[4,768,512]{2,1,0:T(8,128)(2,1)}), bf16[1,768,512]{2,1,0:T(8,128)(2,1)}) %reduce-scatter.7.cloned.1.call-update) | async-done | bytes 786448 | tf_op jit(solution)/shard_map/reduce_scatter | solution.py:256
  612.4 145.1 %all-reduce.10.cloned.1.call-done = (bf16[768,192]{0,1:T(8,128)(2,1)}, bf16[768,192]{0,1:T(8,128)(2,1)}, bf16[768,192]{0,1:T(8,128)(2,1)}, bf16[192,768]{1,0:T(8...) async-done(((bf16[768,192]{0,1:T(8,128)(2,1)}, bf16[768,192]{0,1:T(8,128)(2,1)}, bf16[768,192]{0,1:T(8,128)(2,1)}, ...) | async-done | bytes 3538960 | tf_op jit(solution)/shard_map/psum | solution.py:289
  (447 shorter events, 222.6 us)
Async XLA Ops:
  7.2 202.5 %copy-start = (bf16[512,768]{1,0:T(8,128)(2,1)S(1)}, bf16[512,768]{1,0:T(8,128)(2,1)}, u32[]{:S(2)}) copy-start(bf16[512,768]{1,0:T(8,128)(2,1)} %param.32) | copy-start | bytes 2359300
  7.2 34.5 %all-gather.18.cloned.1.call-start = ((), (), s32[]{:S(2)}) async-start(), calls=%async_computation.19 | async-start | bytes 1474560 | tf_op jit(solution)/shard_map/all_gather | solution.py:170
  7.9 54.3 %all-gather.8.cloned.1.call-start = ((), (), s32[]{:S(2)}) async-start(), calls=%async_computation.8 | async-start | bytes 1966080 | tf_op jit(solution)/shard_map/all_gather | solution.py:181
  10.5 51.7 %copy-start.8 = (bf16[1024,768]{0,1:T(8,128)(2,1)}, bf16[1024,768]{0,1:T(8,128)(2,1)S(1)}, u32[]{:S(2)}) copy-start(bf16[1024,768]{0,1:T(8,128)(2,1)S(1)} %copy.70) | copy-start | bytes 4718596
  39.7 64.5 %all-gather.10.cloned.1.call-start = ((), (), s32[]{:S(2)}) async-start(), calls=%async_computation.9 | async-start | bytes 3932160 | tf_op jit(solution)/shard_map/all_gather | solution.py:167
  40.4 81.9 %all-gather.12.cloned.1.call-start = ((), (), s32[]{:S(2)}) async-start(), calls=%async_computation.10 | async-start | bytes 3932160 | tf_op jit(solution)/shard_map/all_gather | solution.py:168
  41.0 111.3 %all-gather.14.cloned.1.call-start = ((), (), s32[]{:S(2)}) async-start(), calls=%async_computation.11 | async-start | bytes 3932160 | tf_op jit(solution)/shard_map/all_gather | solution.py:169
  67.3 108.6 %copy-start.10 = (bf16[1024,768]{0,1:T(8,128)(2,1)}, bf16[1024,768]{0,1:T(8,128)(2,1)S(1)}, u32[]{:S(2)}) copy-start(bf16[1024,768]{0,1:T(8,128)(2,1)S(1)} %multiply_convert_fusion.1) | copy-start | bytes 4718596
  166.5 34.7 %all-to-all-start.1 = ((bf16[8,96,768]{2,1,0:T(8,128)(2,1)}), bf16[8,96,768]{2,1,0:T(8,128)(2,1)}, u32[]{:S(2)}, u32[]{:S(2)}) async-start(bf16[8,96,768]{2,1,0:T(8,128)(2,1)} %bitcast.292), calls=%async_computation.1 | async-start | bytes 2359296 | tf_op jit(solution)/shard_map/all_to_all | solution.py:205
  172.1 66.4 %reduce-scatter.5.cloned.1.call-start = ((), (), s32[]{:S(2)}) async-start(), calls=%async_computation.12 | async-start | bytes 1966080 | tf_op jit(solution)/shard_map/reduce_scatter | solution.py:215
  209.7 28.8 %copy-start.75 = (bf16[1024,192]{0,1:T(8,128)(2,1)S(1)}, bf16[1024,192]{0,1:T(8,128)(2,1)}, u32[]{:S(2)}) copy-start(bf16[1024,192]{0,1:T(8,128)(2,1)} %param.39) | copy-start | bytes 1179652
  212.1 49.2 %all-gather.16.cloned.1.call-start = ((), (), s32[]{:S(2)}) async-start(), calls=%async_computation.13 | async-start | bytes 1966080 | tf_op jit(solution)/shard_map/all_gather | solution.py:221
  264.5 36.6 %copy-start.21 = (bf16[4,512,768]{2,1,0:T(8,128)(2,1)S(1)}, bf16[4,512,768]{2,1,0:T(8,128)(2,1)}, u32[]{:S(2)}) copy-start(bf16[4,512,768]{2,1,0:T(8,128)(2,1)} %all-gather.14.cloned.1.call-done) | copy-start | bytes 9437188
  264.5 36.6 %copy-start.124 = (f32[768,512]{1,0:T(8,128)S(1)}, f32[768,512]{1,0:T(8,128)}, u32[]{:S(2)}) copy-start(f32[768,512]{1,0:T(8,128)} %get-tuple-element.261) | copy-start | bytes 4718596
  266.2 34.9 %copy-start.118 = (f32[768,512]{1,0:T(8,128)S(1)}, f32[768,512]{1,0:T(8,128)}, u32[]{:S(2)}) copy-start(f32[768,512]{1,0:T(8,128)} %fusion.117) | copy-start | bytes 4718596
  318.3 32.2 %all-to-all-start.3 = ((bf16[8,96,768]{2,1,0:T(8,128)(2,1)}), bf16[8,96,768]{2,1,0:T(8,128)(2,1)}, u32[]{:S(2)}, u32[]{:S(2)}) async-start(bf16[8,96,768]{2,1,0:T(8,128)(2,1)} %bitcast.291), calls=%async_computation.4 | async-start | bytes 2359296 | tf_op jit(solution)/shard_map/all_to_all | solution.py:247
  322.5 73.9 %all-reduce.6.cloned.1.call-start = ((), (), s32[]{:S(2)}) async-start(), calls=%async_computation.14 | async-start | bytes 3145728 | tf_op jit(solution)/shard_map/psum | solution.py:267
  355.6 132.4 %all-reduce.8.cloned.1.call-start = ((), (), s32[]{:S(2)}) async-start(), calls=%async_computation.15 | async-start | bytes 3145728 | tf_op jit(solution)/shard_map/psum | solution.py:283
  358.8 37.7 %copy-start.91 = (f32[1024]{0:T(1024)S(1)}, f32[1024]{0:T(1024)}, u32[]{:S(2)}) copy-start(f32[1024]{0:T(1024)} %copy-done.90) | copy-start | bytes 12292
  358.8 37.7 %copy-start.97 = (f32[768]{0:T(1024)S(1)}, f32[768]{0:T(1024)}, u32[]{:S(2)}) copy-start(f32[768]{0:T(1024)} %param.28) | copy-start | bytes 9220
  444.9 95.1 %reduce-scatter.9.cloned.1.call-start = ((), (), s32[]{:S(2)}) async-start(), calls=%async_computation.17 | async-start | bytes 3932160 | tf_op jit(solution)/shard_map/reduce_scatter | solution.py:256
  449.8 119.5 %reduce-scatter.11.cloned.1.call-start = ((), (), s32[]{:S(2)}) async-start(), calls=%async_computation.18 | async-start | bytes 3932160 | tf_op jit(solution)/shard_map/reduce_scatter | solution.py:256
  458.3 151.6 %reduce-scatter.7.cloned.1.call-start = ((), (), s32[]{:S(2)}) async-start(), calls=%async_computation.16 | async-start | bytes 3932160 | tf_op jit(solution)/shard_map/reduce_scatter | solution.py:256
  465.5 291.9 %all-reduce.10.cloned.1.call-start = ((), (), s32[]{:S(2)}) async-start(), calls=%async_computation.20 | async-start | bytes 7077888 | tf_op jit(solution)/shard_map/psum | solution.py:289
  (121 other events, 500.2 us)
Sparse Core Ops, SparseCore 0:
  9.6 20.1 all-gather.17
  39.8 22.3 all-gather.7
  63.8 28.5 all-gather.9
  93.8 28.5 all-gather.11
  123.7 28.5 all-gather.13
  212.2 26.2 reduce-scatter.4
  241.6 19.6 all-gather.15
  355.7 40.7 all-reduce.5
  445.0 42.8 all-reduce.7
  490.5 38.1 reduce-scatter.8
  531.2 38.0 reduce-scatter.10
  571.9 37.9 reduce-scatter.6
  615.5 141.8 all-reduce.9

commit v2 on v1

--- a/solution.py
+++ b/solution.py
@@ -1,12 +1,237 @@
+import functools
+
 import jax
 import jax.numpy as jnp
+import numpy as np
 from jax import lax
+from jax.experimental import pallas as pl
+from jax.experimental.pallas import tpu as pltpu
 from jax.sharding import PartitionSpec as P
 
 HD = 64
+F32, BF16 = jnp.float32, jnp.bfloat16
+MESH = pl.DeviceIdType.MESH
 
 
 eps_norm = 1e-06
+
+
+def rope_rows(length, heads):
+    half = HD // 2
+    freqs = (10000.0 ** (-2.0 * np.arange(half) / HD)).astype(np.float32)
+    angles = np.arange(length, dtype=np.float32)[:, None] * freqs[None, :]
+    cosine, sine = np.cos(angles), np.sin(angles)
+    return (
+        np.tile(np.concatenate([cosine, cosine], axis=1), (1, heads)).astype(np.float32),
+        np.tile(np.concatenate([-sine, sine], axis=1), (1, heads)).astype(np.float32),
+    )
+
+
+def peer_of(t, step):
+    if step == 1:
+        return t + 1 - 2 * lax.rem(t, 2)
+    return lax.rem(t + 2, 4)
+
+
+def greet(peers):
+    barrier = pltpu.get_barrier_semaphore()
+    for peer in peers:
+        pl.semaphore_signal(barrier, inc=1, device_id=peer, device_id_type=MESH)
+    pl.semaphore_wait(barrier, len(peers))
+
+
+def mm(a, b):
+    return lax.dot_general(a, b, (((1,), (0,)), ((), ())), preferred_element_type=F32)
+
+
+def mm_nt(a, b):
+    return lax.dot_general(a, b, (((1,), (1,)), ((), ())), preferred_element_type=F32)
+
+
+def mm_tn(a, b):
+    return lax.dot_general(a, b, (((0,), (0,)), ((), ())), preferred_element_type=F32)
+
+
+def swap_halves(width):
+    row = lax.broadcasted_iota(jnp.int32, (width, width), 0)
+    col = lax.broadcasted_iota(jnp.int32, (width, width), 1)
+    half = HD // 2
+    other = jnp.where(lax.rem(col, HD) < half, col + half, col - half)
+    return (row == other).astype(F32).astype(BF16)
+
+
+def head_mask(rows, width, head):
+    col = lax.broadcasted_iota(jnp.int32, (rows, width), 1)
+    return (col >= head * HD) & (col < (head + 1) * HD)
+
+
+def only(value, head):
+    keep = head_mask(value.shape[0], value.shape[1], head)
+    return jnp.where(keep, value, jnp.zeros_like(value))
+
+
+def attend_kernel(
+    block,
+    hidden,
+    gain_one,
+    w_query,
+    w_key,
+    w_value,
+    w_out,
+    gain_two,
+    cosine,
+    sine,
+    seg_col,
+    seg_row,
+    query,
+    keys,
+    values,
+    summary,
+    residual,
+    normed_two,
+    mixed_all,
+    out_all,
+    send_sem,
+    recv_sem,
+    wsend_sem,
+    wrecv_sem,
+    copy_sem,
+):
+    length = hidden.shape[0]
+    lanes = w_query.shape[1]
+    heads = lanes // HD
+    blocks = length // block
+    e, t = lax.axis_index("expert"), lax.axis_index("tensor")
+    beside, across = peer_of(t, 1), peer_of(t, 2)
+    greet([(e, beside), (e, across)])
+
+    def share(src, dst, device, sem):
+        return pltpu.make_async_remote_copy(
+            src_ref=src,
+            dst_ref=dst,
+            send_sem=sem[0],
+            recv_sem=sem[1],
+            device_id=(e, device),
+            device_id_type=MESH,
+        )
+
+    def weight(k):
+        src = w_out if k < 2 else out_all.at[across]
+        dst = out_all.at[t] if k < 2 else out_all.at[across]
+        return share(src, dst, across if k == 0 else beside, (wsend_sem.at[k], wrecv_sem.at[k]))
+
+    own = pltpu.make_async_copy(w_out, out_all.at[t], copy_sem)
+    own.start()
+    weight(0).start()
+    weight(1).start()
+
+    def piece(i, k):
+        rows = pl.ds(i * block, block)
+        slot = t if k < 2 else across
+        ref = mixed_all.at[slot, rows]
+        return share(
+            ref, ref, across if k == 0 else beside, (send_sem.at[i, k], recv_sem.at[i, k])
+        )
+
+    for i in range(blocks):
+        rows = pl.ds(i * block, block)
+        inputs = hidden[rows, :].astype(F32)
+        scale = lax.rsqrt(jnp.mean(inputs * inputs, axis=-1, keepdims=True) + eps_norm)
+        normed = (inputs * scale * gain_one[...]).astype(BF16)
+        values[rows, :] = mm(normed, w_value[...]).astype(BF16)
+        swap = swap_halves(lanes)
+        for weight_ref, made in ((w_query, query), (w_key, keys)):
+            plain = mm(normed, weight_ref[...])
+            swapped = mm(normed, mm(weight_ref[...], swap).astype(BF16))
+            made[rows, :] = (plain * cosine[rows, :] + swapped * sine[rows, :]).astype(BF16)
+
+    def project(i):
+        rows = pl.ds(i * block, block)
+        piece(i, 1).wait_recv()
+        piece(i, 2).wait_recv()
+        total = hidden[rows, :].astype(F32)
+        for m in range(4):
+            total = total + mm(mixed_all[m, rows, :], out_all[m])
+        residual[rows, :] = total
+        scale = lax.rsqrt(jnp.mean(total * total, axis=-1, keepdims=True) + eps_norm)
+        normed_two[rows, :] = (total * scale * gain_two[...]).astype(BF16)
+
+    for i in range(blocks):
+        rows = pl.ds(i * block, block)
+        reach = (i + 1) * block
+        key_at = lax.broadcasted_iota(jnp.int32, (reach, block), 0)
+        query_at = lax.broadcasted_iota(jnp.int32, (reach, block), 1) + i * block
+        allowed = (seg_col[0:reach, :] == seg_row[:, rows]) & (key_at <= query_at)
+        q_block = query[rows, :] * (HD ** (-0.5))
+        mixed = jnp.zeros((block, lanes), F32)
+        for h in range(heads):
+            scores = mm_nt(keys[0:reach, :], only(q_block, h))
+            scores = jnp.where(allowed, scores, -1e30)
+            top = jnp.max(scores, axis=0, keepdims=True)
+            expo = jnp.exp(scores - top)
+            total = jnp.sum(expo, axis=0, keepdims=True)
+            prob = (expo * (1.0 / total)).astype(BF16)
+            mixed = mixed + mm_tn(prob, only(values[0:reach, :], h))
+            summary[h : h + 1, rows] = top + jnp.log(total)
+        mixed_all[t, rows, :] = mixed.astype(BF16)
+        piece(i, 0).start()
+        piece(i, 1).start()
+        if i == 0:
+            weight(0).wait_recv()
+            weight(2).start()
+        else:
+            piece(i - 1, 0).wait_recv()
+            piece(i - 1, 2).start()
+        if i == 1:
+            own.wait()
+            weight(1).wait_recv()
+            weight(2).wait_recv()
+        if i >= 2:
+            project(i - 2)
+    piece(blocks - 1, 0).wait_recv()
+    piece(blocks - 1, 2).start()
+    for i in range(max(blocks - 2, 0), blocks):
+        project(i)
+    for i in range(blocks):
+        for k in range(3):
+            piece(i, k).wait_send()
+    for k in range(3):
+        weight(k).wait_send()
+
+
+def attend(hidden, gain_one, w_query, w_key, w_value, w_out, gain_two, tables, seg_col, seg_row):
+    length, width = hidden.shape
+    lanes = w_query.shape[1]
+    block = length // 4
+    shape = jax.ShapeDtypeStruct
+    vmem = pl.BlockSpec(memory_space=pltpu.VMEM)
+    dma = pltpu.SemaphoreType.DMA
+    return pl.pallas_call(
+        functools.partial(attend_kernel, block),
+        out_shape=(
+            shape((length, lanes), BF16),
+            shape((length, lanes), BF16),
+            shape((length, lanes), BF16),
+            shape((8, length), F32),
+            shape((length, width), F32),
+            shape((length, width), BF16),
+            shape((4, length, lanes), BF16),
+        ),
+        in_specs=[vmem] * 11,
+        out_specs=(vmem,) * 7,
+        scratch_shapes=[
+            pltpu.VMEM((4, lanes, width), BF16),
+            dma((4, 3)),
+            dma((4, 3)),
+            dma((3,)),
+            dma((3,)),
+            dma,
+        ],
+        compiler_params=pltpu.CompilerParams(
+            collective_id=1, has_side_effects=True, vmem_limit_bytes=56 * 2**20
+        ),
+        name="attend",
+    )(hidden, gain_one, w_query, w_key, w_value, w_out, gain_two, *tables, seg_col, seg_row)
 
 
 def rope_tables(length, head_dim):
@@ -161,28 +386,31 @@
     block = min(512, length)
     f32, bf16 = jnp.float32, jnp.bfloat16
 
-    def mm(a, b):
-        return jnp.dot(a, b, preferred_element_type=f32)
-
     gate_all = lax.all_gather(expert_gate[0], "tensor", axis=0)
     up_all = lax.all_gather(expert_up[0], "tensor", axis=0)
     down_all = lax.all_gather(expert_down[0], "tensor", axis=0)
-    out_all = lax.all_gather(w_out, "tensor", axis=0)
-
+
+    tables = rope_rows(length, local_heads)
+    query_rows, keys_rows, values_rows, summary_rows, residual, normed_two, mixed_all = attend(
+        hidden_in,
+        norm_attn[None],
+        w_query,
+        w_key,
+        w_value,
+        w_out,
+        norm_ffn[None],
+        tables,
+        segment[:, None],
+        segment[None],
+    )
+    mixed_low = lax.dynamic_index_in_dim(mixed_all, me, 0, keepdims=False)
+    query, keys, values = (split_heads(a, local_heads) for a in (query_rows, keys_rows, values_rows))
+    summary = summary_rows[:local_heads]
     inputs = hidden_in.astype(f32)
     scale_one = lax.rsqrt(jnp.mean(inputs * inputs, axis=-1, keepdims=True) + eps_norm)
     normed_one = (inputs * scale_one * norm_attn).astype(bf16)
+    scale_two = lax.rsqrt(jnp.mean(residual * residual, axis=-1, keepdims=True) + eps_norm)
     cosine, sine = rope_tables(length, HD)
-    query = rotate(split_heads(mm(normed_one, w_query), local_heads), cosine, sine).astype(bf16)
-    keys = rotate(split_heads(mm(normed_one, w_key), local_heads), cosine, sine).astype(bf16)
-    values = split_heads(mm(normed_one, w_value), local_heads).astype(bf16)
-    mixed, summary = attend_forward(query, keys, values, segment, block)
-    mixed_low = merge_heads(mixed).astype(bf16)
-    mixed_all = lax.all_gather(mixed_low, "tensor", axis=0)
-    attention = jnp.einsum("mth,mhd->td", mixed_all, out_all, preferred_element_type=f32)
-    residual = inputs + attention
-    scale_two = lax.rsqrt(jnp.mean(residual * residual, axis=-1, keepdims=True) + eps_norm)
-    normed_two = (residual * scale_two * norm_ffn).astype(bf16)
     logits = mm(normed_two, w_router)
     onehot = (routes[:, :, None] == jnp.arange(experts, dtype=jnp.int32)[None, None, :]).astype(f32)
     chosen = jnp.sum(logits[:, None, :] * onehot, axis=2)

time: 786 us -> 755 us (0.961)
  Pallas kernels: 0 us -> 47.1 us
  waiting for transfers between devices: 386 us -> 349 us
  blocking collectives: 110 us -> 75.5 us
  matrix products: 150 us -> 134 us
  local copies, waits for them, and re-layouts: 29.6 us -> 40.4 us
    pallas_call x0 -> x1, Pallas kernels: none -> 47.1 us  [attend(): pl.pallas_call(functools.partial(attend_kernel, block), out_shape=(shape(...]
    all_to_all x1 -> x0, blocking collectives: 34.9 us -> none  [body(): lax.all_to_all(grad_out_rows.reshape(groups, share, width), 'expert', spl...]
    reduce_scatter x1 -> x0, waiting for transfers between devices: 26.4 us -> none  [body(): lax.psum_scatter((side_part + mixture).astype(bf16), 'tensor', scatter_di...]
    all_to_all x0 -> x1, waiting for transfers between devices: none -> 25.6 us  [body(): lax.all_to_all(grad_out_rows.reshape(groups, share, width), 'expert', spl...]
    unnamed x13 -> x12, waiting for transfers between devices: 2.56 us -> 27.5 us
    all_gather x1, waiting for transfers between devices: 22.1 us -> 1.35 us  [body(): down_all = lax.all_gather(expert_down[0], 'tensor', axis=0)]
    all_gather x2 -> x0, waiting for transfers between devices: 20.5 us -> none  [the longest x1 20.5 us: body(): mixed_all = lax.all_gather(mixed_low, 'tensor', axis=0)]
    dot_general x68 -> x62, matrix products: 122 us -> 112 us  [mm(): lax.dot_general(a, b, (((1,), (0,)), ((), ())), preferred_element_type=F32)]
  transfers between devices with their start and end apart: 15 -> 14, of which waited for: 12 -> 11; matrix products, arithmetic and copies ran while one was open for 16% -> 15% of each run, Pallas kernels for 0% -> 6%
where the time goes in v2:
time: 755 us; the launch traced here: 744 us
  waiting for transfers between devices  349 us (46%)
  matrix products  134 us (18%)
  blocking collectives  75.5 us (10%)
  other arithmetic  57.2 us (8%)
  Pallas kernels  47.1 us (6%)
  local copies, waits for them, and re-layouts  40.4 us (5%)
  between operations  19.1 us (3%)
  starting transfers between devices  16.2 us (2%)
    psum x1, waiting for transfers between devices, body(): lax.psum(tuple((g.astype(bf16) for g in (grad_w_query, grad_w_key, grad_w...  145 us
    dot_general x62, matrix products, mm(): lax.dot_general(a, b, (((1,), (0,)), ((), ())), preferred_element_type=F32)  112 us
    reduce_scatter x3, waiting for transfers between devices, reduced(): return lax.psum_scatter(jnp.stack(parts), 'tensor', scatter_dimension=0)  63 us
    pallas_call x1, Pallas kernels, attend(): pl.pallas_call(functools.partial(attend_kernel, block), out_shape=(shape(...  47.1 us
    psum x1, blocking collectives, body(): lax.psum((jnp.sum(error * error), jnp.sum(valid) / members, grad_router,...  40.3 us
    all_to_all x1, blocking collectives, body(): lax.all_to_all(outgoing, 'expert', split_axis=0, concat_axis=0, tiled=True)  35.2 us
    psum x1, waiting for transfers between devices, body(): grad_normed = lax.psum(grad_normed.astype(bf16), 'tensor').astype(f32)  29.9 us
    unnamed x12, waiting for transfers between devices  27.5 us
  transfers between devices with their start and end apart: 14, of which 11 were waited for; matrix products, arithmetic and copies ran while one was open for 15% of the time, Pallas kernels for 6%

profile of v2, /device:TPU:0, one launch (start us, length us, event | category | flops | bytes accessed | tf_op | source)
XLA Modules:
  0.0 743.7 jit_solution(16758874376940888632)
XLA Ops:
  14.6 47.1 %attend.1 = (bf16[1024,192]{1,0:T(8,128)(2,1)}, bf16[1024,192]{1,0:T(8,128)(2,1)}, bf16[1024,192]{1,0:T(8,128)(2,1)}, f32[8,1024]{1,0:T(8,128)}, f32[1024,768]{1...) custom-call(bf16[1024,768]{1,0:T(8,128)(2,1)} %hidden.1, f32[1,768]{1,0:T(1,128)} %broadcast_in_dim.31.gain_one, ...), custom_call_target="tpu_custom_call" | custom-call | tf_op jit(solution)/shard_map/attend/pallas_call | solution.py:209
  65.0 35.2 %all_to_all.20 = bf16[8,96,768]{2,1,0:T(8,128)(2,1)S(1)} all-to-all(bf16[8,96,768]{2,1,0:T(8,128)(2,1)S(1)} %bitcast.280), channel_id=1, replica_groups=mesh['expert'=8,'tensor'=4] {'expert'}, dimensions={0} | all-to-all | bytes 2359296 | tf_op jit(solution)/shard_map/all_to_all | solution.py:423
  109.5 3.8 multiply_convert_fusion.16
  129.8 5.6 all-to-all-start.1
  144.8 19.7 %all-to-all-done.1 = bf16[8,96,768]{2,1,0:T(8,128)(2,1)S(1)} async-done(((bf16[8,96,768]{2,1,0:T(8,128)(2,1)}), bf16[8,96,768]{2,1,0:T(8,128)(2,1)S(1)}, u32[]{:S(2)}, u32[]{:S(2)}) %all-to-all-start.1) | async-done | bytes 1179680 | tf_op jit(solution)/shard_map/all_to_all | solution.py:433
  175.9 25.3 %reduce-scatter.13.cloned.1.call-done = bf16[192,1024]{1,0:T(8,128)(2,1)} async-done(((bf16[768,1024]{1,0:T(8,128)(2,1)}), bf16[192,1024]{1,0:T(8,128)(2,1)}) %reduce-scatter.13.cloned.1.call-update) | async-done | bytes 393232
  206.8 19.8 %all-gather.11.cloned.1.call-done = bf16[1024,768]{0,1:T(8,128)(2,1)} async-done(((bf16[1024,192]{0,1:T(8,128)(2,1)}), bf16[1024,768]{0,1:T(8,128)(2,1)}) %all-gather.11.cloned.1.call-update) | async-done | bytes 1572880 | tf_op jit(solution)/shard_map/all_gather | solution.py:449
  233.5 5.7 all-to-all-start.2
  242.6 25.6 %all-to-all-done.2 = bf16[8,96,768]{2,1,0:T(8,128)(2,1)S(1)} async-done(((bf16[8,96,768]{2,1,0:T(8,128)(2,1)}), bf16[8,96,768]{2,1,0:T(8,128)(2,1)S(1)}, u32[]{:S(2)}, u32[]{:S(2)}) %all-to-all-start.2) | async-done | bytes 1179680 | tf_op jit(solution)/shard_map/all_to_all | solution.py:456
  268.2 3.9 multiply_convert_fusion.5
  287.2 3.7 all-to-all-start.3
  291.2 3.8 fusion.30
  302.9 16.7 %all-to-all-done.3 = bf16[8,96,768]{2,1,0:T(8,128)(2,1)S(1)} async-done(((bf16[8,96,768]{2,1,0:T(8,128)(2,1)}), bf16[8,96,768]{2,1,0:T(8,128)(2,1)S(1)}, u32[]{:S(2)}, u32[]{:S(2)}) %all-to-all-start.3) | async-done | bytes 1179680 | tf_op jit(solution)/shard_map/all_to_all | solution.py:475
  335.6 29.9 %all-reduce.6.cloned.1.call-done = bf16[1024,768]{1,0:T(8,128)(2,1)} async-done(((bf16[1024,768]{1,0:T(8,128)(2,1)}), bf16[1024,768]{1,0:T(8,128)(2,1)}) %all-reduce.6.cloned.1.call-update) | async-done | bytes 1572880 | tf_op jit(solution)/shard_map/psum | solution.py:495
  365.5 3.6 fusion.23
  373.6 34.0 %while.15 = (s32[]{:T(128)}, f32[3,1024,64]{1,2,0:T(8,128)S(1)}, f32[3,1024,64]{1,2,0:T(8,128)S(1)}, f32[2,3,512,64]{2,3,1,0:T(8,128)}, s32[2]{0:T(128)S(1)}, /*...) while((s32[]{:T(128)}, f32[3,1024,64]{1,2,0:T(8,128)S(1)}, ...), condition=%wide.region_18.19_spmd.clone, body=%wide.region_16.18_spmd.clone.sunk | while | flops 1025014784 | bytes 60076316 | solution.py:350
  380.2 4.4 multiply_reduce_fusion.5
  397.0 4.4 multiply_reduce_fusion.5
  456.7 5.1 fusion.27
  461.8 40.3 %all-reduce = (f32[]{:T(128)}, f32[]{:T(128)}, f32[768]{0:T(1024)S(1)}, f32[768]{0:T(1024)S(1)}, f32[768,8]{0,1:T(8,128)S(1)}) all-reduce(f32[]{:T(128)} %get-tuple-element.235, f32[]{:T(128)S(6)} %div.100, f32[768]{0:T(1024)S(1)} %broadcast_multiply_fusion.4, ...), channel_id=1, replica_groups=mesh['expert'=8,'tensor'=4] {'expert','tensor'}, use_global_device_ids=true, to_apply=%region_5.6 | all-reduce | flops 7682 | bytes 61456 | tf_op jit(solution)/shard_map/psum | solution.py:520
  503.4 3.7 fusion.77
  513.4 24.8 %reduce-scatter.11.cloned.1.call-done = bf16[1,512,768]{2,1,0:T(8,128)(2,1)} async-done(((bf16[4,512,768]{2,1,0:T(8,128)(2,1)}), bf16[1,512,768]{2,1,0:T(8,128)(2,1)}) %reduce-scatter.11.cloned.1.call-update) | async-done | bytes 786448 | tf_op jit(solution)/shard_map/reduce_scatter | solution.py:484
  540.6 38.1 %reduce-scatter.7.cloned.1.call-done = bf16[1,768,512]{2,1,0:T(8,128)(2,1)} async-done(((bf16[4,768,512]{2,1,0:T(8,128)(2,1)}), bf16[1,768,512]{2,1,0:T(8,128)(2,1)}) %reduce-scatter.7.cloned.1.call-update) | async-done | bytes 786448 | tf_op jit(solution)/shard_map/reduce_scatter | solution.py:484
  581.2 145.0 %all-reduce.10.cloned.1.call-done = (bf16[768,192]{0,1:T(8,128)(2,1)}, bf16[768,192]{0,1:T(8,128)(2,1)}, bf16[768,192]{0,1:T(8,128)(2,1)}, bf16[192,768]{1,0:T(8...) async-done(((bf16[768,192]{0,1:T(8,128)(2,1)}, bf16[768,192]{0,1:T(8,128)(2,1)}, bf16[768,192]{0,1:T(8,128)(2,1)}, ...) | async-done | bytes 3538960 | tf_op jit(solution)/shard_map/psum | solution.py:517
  (406 shorter events, 204.7 us)
Async XLA Ops:
  7.2 162.8 %copy-start = (bf16[512,768]{1,0:T(8,128)(2,1)S(1)}, bf16[512,768]{1,0:T(8,128)(2,1)}, u32[]{:S(2)}) copy-start(bf16[512,768]{1,0:T(8,128)(2,1)} %param.32) | copy-start | bytes 2359300
  7.3 92.9 %all-gather.5.cloned.1.call-start = ((), (), s32[]{:S(2)}) async-start(), calls=%async_computation.8 | async-start | bytes 3932160 | tf_op jit(solution)/shard_map/all_gather | solution.py:389
  8.0 101.5 %all-gather.7.cloned.1.call-start = ((), (), s32[]{:S(2)}) async-start(), calls=%async_computation.9 | async-start | bytes 3932160 | tf_op jit(solution)/shard_map/all_gather | solution.py:390
  8.8 109.3 %all-gather.9.cloned.1.call-start = ((), (), s32[]{:S(2)}) async-start(), calls=%async_computation.10 | async-start | bytes 3932160 | tf_op jit(solution)/shard_map/all_gather | solution.py:391
  9.6 52.1 %copy-start.95 = (s32[1024,1]{0,1:T(1,128)}, s32[1024,1]{0,1:T(1,128)S(1)}, u32[]{:S(2)}) copy-start(s32[1024,1]{0,1:T(1,128)S(1)} %get-tuple-element.257) | copy-start | bytes 12292
  9.6 52.1 %copy-start.99 = (s32[1024,1]{0,1:T(1,128)}, s32[1024,1]{0,1:T(1,128)S(1)}, u32[]{:S(2)}) copy-start(s32[1024,1]{0,1:T(1,128)S(1)} %get-tuple-element.258) | copy-start | bytes 12292
  100.2 24.8 %copy-start.24 = (bf16[8,96,768]{2,1,0:T(8,128)(2,1)}, bf16[8,96,768]{2,1,0:T(8,128)(2,1)S(1)}, u32[]{:S(2)}) copy-start(bf16[8,96,768]{2,1,0:T(8,128)(2,1)S(1)} %all_to_all.20) | copy-start | bytes 3538948
  129.8 34.6 %all-to-all-start.1 = ((bf16[8,96,768]{2,1,0:T(8,128)(2,1)}), bf16[8,96,768]{2,1,0:T(8,128)(2,1)S(1)}, u32[]{:S(2)}, u32[]{:S(2)}) async-start(bf16[8,96,768]{2,1,0:T(8,128)(2,1)} %bitcast.19), calls=%async_computation.1 | async-start | bytes 2359296 | tf_op jit(solution)/shard_map/all_to_all | solution.py:433
  135.5 65.7 %reduce-scatter.13.cloned.1.call-start = ((), (), s32[]{:S(2)}) async-start(), calls=%async_computation.17 | async-start | bytes 1966080
  174.7 51.9 %all-gather.11.cloned.1.call-start = ((), (), s32[]{:S(2)}) async-start(), calls=%async_computation.11 | async-start | bytes 1966080 | tf_op jit(solution)/shard_map/all_gather | solution.py:449
  206.7 21.5 %copy-start.92 = (f32[1024,1]{0,1:T(1,128)S(1)}, f32[1024,1]{0,1:T(1,128)}, u32[]{:S(2)}) copy-start(f32[1024,1]{0,1:T(1,128)} %get-tuple-element.256) | copy-start | bytes 12292
  206.8 21.5 %copy-start.100 = (s32[1024,1]{0,1:T(1,128)S(1)}, s32[1024,1]{0,1:T(1,128)}, u32[]{:S(2)}) copy-start(s32[1024,1]{0,1:T(1,128)} %copy-done.99) | copy-start | bytes 12292
  228.3 62.8 %copy-start.5 = (bf16[1024,768]{1,0:T(8,128)(2,1)}, bf16[1024,768]{1,0:T(8,128)(2,1)S(1)}, u32[]{:S(2)}) copy-start(bf16[1024,768]{1,0:T(8,128)(2,1)S(1)} %copy.101) | copy-start | bytes 4718596
  233.5 34.6 %all-to-all-start.2 = ((bf16[8,96,768]{2,1,0:T(8,128)(2,1)}), bf16[8,96,768]{2,1,0:T(8,128)(2,1)S(1)}, u32[]{:S(2)}, u32[]{:S(2)}) async-start(bf16[8,96,768]{2,1,0:T(8,128)(2,1)} %bitcast.279), calls=%async_computation.2 | async-start | bytes 2359296 | tf_op jit(solution)/shard_map/all_to_all | solution.py:456
  287.2 32.4 %all-to-all-start.3 = ((bf16[8,96,768]{2,1,0:T(8,128)(2,1)}), bf16[8,96,768]{2,1,0:T(8,128)(2,1)S(1)}, u32[]{:S(2)}, u32[]{:S(2)}) async-start(bf16[8,96,768]{2,1,0:T(8,128)(2,1)} %bitcast.24), calls=%async_computation.3 | async-start | bytes 2359296 | tf_op jit(solution)/shard_map/all_to_all | solution.py:475
  290.9 74.6 %all-reduce.6.cloned.1.call-start = ((), (), s32[]{:S(2)}) async-start(), calls=%async_computation.12 | async-start | bytes 3145728 | tf_op jit(solution)/shard_map/psum | solution.py:495
  295.1 26.3 %copy-start.76 = (bf16[1024,8]{0,1:T(8,128)(2,1)}, bf16[1024,8]{0,1:T(8,128)(2,1)S(1)}, u32[]{:S(2)}) copy-start(bf16[1024,8]{0,1:T(8,128)(2,1)S(1)} %select_reduce_fusion) | copy-start | bytes 49156
  324.3 132.3 %all-reduce.8.cloned.1.call-start = ((), (), s32[]{:S(2)}) async-start(), calls=%async_computation.13 | async-start | bytes 3145728 | tf_op jit(solution)/shard_map/psum | solution.py:511
  333.9 31.6 %copy-start.85 = (f32[768]{0:T(1024)S(1)}, f32[768]{0:T(1024)}, u32[]{:S(2)}) copy-start(f32[768]{0:T(1024)} %param.28) | copy-start | bytes 9220
  333.9 31.6 %copy-start.86 = (f32[1024]{0:T(1024)S(1)}, f32[1024]{0:T(1024)}, u32[]{:S(2)}) copy-start(f32[1024]{0:T(1024)} %add_rsqrt_fusion.1) | copy-start | bytes 12292
  413.6 97.2 %reduce-scatter.9.cloned.1.call-start = ((), (), s32[]{:S(2)}) async-start(), calls=%async_computation.15 | async-start | bytes 3932160 | tf_op jit(solution)/shard_map/reduce_scatter | solution.py:484
  420.2 118.0 %reduce-scatter.11.cloned.1.call-start = ((), (), s32[]{:S(2)}) async-start(), calls=%async_computation.16 | async-start | bytes 3932160 | tf_op jit(solution)/shard_map/reduce_scatter | solution.py:484
  427.8 150.9 %reduce-scatter.7.cloned.1.call-start = ((), (), s32[]{:S(2)}) async-start(), calls=%async_computation.14 | async-start | bytes 3932160 | tf_op jit(solution)/shard_map/reduce_scatter | solution.py:484
  435.0 291.3 %all-reduce.10.cloned.1.call-start = ((), (), s32[]{:S(2)}) async-start(), calls=%async_computation.18 | async-start | bytes 7077888 | tf_op jit(solution)/shard_map/psum | solution.py:517
  (107 other events, 351.0 us)
Sparse Core Ops, SparseCore 0:
  9.7 47.7 all-gather.4
  59.0 28.8 all-gather.6
  89.5 28.5 all-gather.8
  174.8 26.3 reduce-scatter.12
  206.9 19.6 all-gather.10
  324.4 40.9 all-reduce.5
  413.7 42.8 all-reduce.7
  459.4 38.2 reduce-scatter.8
  500.2 37.9 reduce-scatter.10
  540.7 37.9 reduce-scatter.6
  584.4 141.8 all-reduce.9
